TPU v7x, 32 devices: a whole 2x2x4 slice. The times are simulated.
32 devices in a mesh: tm: 8 (over y, x, core), batch: 4 (over z).
Axes of the slice: x: 2, y: 2, z: 4, core: 2. Of those that a mesh axis runs over, the one named last changes fastest.
Arguments:
- rgb_maps: bfloat16 [16, 64, 16, 16, 128], P('batch', 'tm'), may hold values from -6 to 6
- flow_maps: bfloat16 [16, 64, 16, 16, 128], P('batch', 'tm'), may hold values from -6 to 6
- in_weights: bfloat16 [2, 1152, 128], replicated, may hold values from -0.1875 to 0.1875
- out_weights: bfloat16 [2, 1152, 128], replicated, may hold values from -0.1875 to 0.1875
- decay: float32 [2, 64, 128], P(None, 'tm'), may hold values from 0 to 1, as said below
- skip: float32 [2, 128], replicated, may hold values from 0.5 to 1.5
- proj_in: float32 [128, 2048], replicated, may hold values from -0.5 to 0.5
- proj_gain: float32 [2048], replicated, may hold values from 0.1 to 1.9
- proj_out: bfloat16 [2048, 2048], replicated, may hold values from -0.125 to 0.125
Outputs:
- grad_in: float32 [2, 1152, 128], replicated
- grad_out: float32 [2, 1152, 128], replicated
Inputs may be any that keep to these rules, and one draw needn't show every extreme that they name: Every entry of decay is a retention factor between 0 and 1.
All inputs are finite; a program needn't handle non-finite values.
Results may differ from a plain program's by a relative error of at most 0.015.
The roundings to bfloat16 on the way count: a program that leaves them out, or rounds other values in their place, can miss the bound.
Values may be sent and summed in bfloat16 or wider, within the bound.
A program may use at most 256 MiB of HBM per device.

v0:
```python
import jax
import jax.numpy as jnp
from jax import lax
from jax.sharding import PartitionSpec as P

LAMBDA_OFF = 0.0051
EPSILON = 1e-05
HIGHEST = lax.Precision.HIGHEST


def prefix(x, axis, combine, identity, reverse):
    peers, here = (lax.axis_size(axis), lax.axis_index(axis))
    everything = jax.tree.map(lambda part: lax.all_gather(part, axis), x)
    start = jax.tree.map(
        lambda part, zero: jnp.broadcast_to(jnp.asarray(zero, part.dtype), part.shape), x, identity
    )

    def lap(k, before):
        at = peers - 1 - k if reverse else k
        reached = at > here if reverse else at < here
        new = combine(before, jax.tree.map(lambda part: part[at], everything))
        return jax.tree.map(lambda a, b: jnp.where(reached, a, b), new, before)

    return lax.fori_loop(0, peers, lap, start)


def patches(feature_maps, flip_sign):
    map_side = feature_maps.shape[-2]
    padding = [(0, 0)] * (feature_maps.ndim - 3) + [(1, 1), (1, 1), (0, 0)]
    padded = jnp.pad(feature_maps, padding)
    pieces = []
    for row_off in range(3):
        for col_off in range(3):
            top_row = 1 + flip_sign * (row_off - 1)
            left_col = 1 + flip_sign * (col_off - 1)
            pieces.append(
                padded[..., top_row : top_row + map_side, left_col : left_col + map_side, :]
            )
    return jnp.concatenate(pieces, axis=-1)


def convolve(feature_maps, weights, flip_sign):
    stacked = patches(feature_maps, flip_sign)
    flat = stacked.reshape(-1, stacked.shape[-1])
    result = jnp.dot(flat, weights, preferred_element_type=jnp.float32)
    return result.reshape(feature_maps.shape[:-1] + (weights.shape[1],))


def flipped(weights):
    channels = weights.shape[1]
    return weights.reshape(9, channels, channels).transpose(0, 2, 1).reshape(9 * channels, channels)


def weight_product(feature_maps, grads):
    stacked = patches(feature_maps, 1)
    flat = stacked.reshape(-1, stacked.shape[-1])
    return lax.dot_general(
        flat,
        grads.reshape(-1, grads.shape[-1]),
        (((0,), (0,)), ((), ())),
        preferred_element_type=jnp.float32,
    )


def silu_grad(values):
    sigma = jax.nn.sigmoid(values)
    return sigma * (1.0 + values * (1.0 - sigma))


def compose(earlier, latter):
    return (earlier[0] * latter[0], latter[0] * earlier[1] + latter[1])


def compose_pair(earlier, latter):
    first_view = compose((earlier[0], earlier[1]), (latter[0], latter[1]))
    second_view = compose((earlier[2], earlier[3]), (latter[2], latter[3]))
    return (first_view[0], first_view[1], second_view[0], second_view[1])


def local_states(view_maps, in_w, decays):
    inputs = convolve(view_maps, in_w, 1).astype(jnp.bfloat16)
    frames_here = view_maps.shape[1]
    carried = jnp.zeros(view_maps.shape[:1] + view_maps.shape[2:], jnp.float32)
    collected = []
    for frame_idx in range(frames_here):
        carried = decays[frame_idx] * carried + inputs[:, frame_idx].astype(jnp.float32)
        collected.append(carried)
    return (inputs, jnp.stack(collected, axis=1), jnp.prod(decays, axis=0), carried)


def finish_states(inputs, partial_states, decays, incoming, out_w, skip_v):
    running = jnp.cumprod(decays, axis=0)
    states = partial_states + running[None, :, None, None, :] * incoming[:, None]
    states_b = states.astype(jnp.bfloat16)
    mixed_out = convolve(states_b, out_w, 1) + skip_v * inputs.astype(jnp.float32)
    pooled_part = jnp.sum(jax.nn.silu(mixed_out), axis=(1, 2, 3))
    return (states_b, mixed_out, pooled_part)


def local_adjoint(dpool, mixed_out, states_b, decays, out_w, cell_count):
    dmix = dpool[:, None, None, None, :] / cell_count * silu_grad(mixed_out)
    dmix_b = dmix.astype(jnp.bfloat16)
    out_grad = weight_product(states_b, dmix_b)
    from_out = convolve(dmix_b, flipped(out_w), -1)
    frames_here = mixed_out.shape[1]
    adjoint_list = [None] * frames_here
    carried = from_out[:, frames_here - 1]
    adjoint_list[frames_here - 1] = carried
    for frame_idx in range(frames_here - 2, -1, -1):
        carried = from_out[:, frame_idx] + decays[frame_idx + 1] * carried
        adjoint_list[frame_idx] = carried
    partial_adjoint = jnp.stack(adjoint_list, axis=1)
    return (dmix, out_grad, partial_adjoint, decays[0] * partial_adjoint[:, 0])


def finish_adjoint(view_maps, dmix, partial_adjoint, decays, incoming, skip_v):
    reversed_prod = jnp.cumprod(decays[::-1], axis=0)[::-1]
    after_prod = jnp.concatenate(
        [reversed_prod[1:], jnp.ones((1, decays.shape[1]), jnp.float32)], axis=0
    )
    adjoint = partial_adjoint + after_prod[None, :, None, None, :] * incoming[:, None]
    dinput = (adjoint + skip_v * dmix).astype(jnp.bfloat16)
    return weight_product(view_maps, dinput)


def barlow_grads(corr_rows, first_row):
    row_ids = jnp.arange(corr_rows.shape[0]) + first_row
    eye_mask = row_ids[:, None] == jnp.arange(corr_rows.shape[1])[None, :]
    return jnp.where(eye_mask, -2.0 * (1.0 - corr_rows), 2.0 * LAMBDA_OFF * corr_rows)


def per_device(
    rgb_maps, flow_maps, in_weights, out_weights, decay, skip, proj_in, proj_gain, proj_out
):
    channels = rgb_maps.shape[-1]
    state_shape = rgb_maps.shape[:1] + rgb_maps.shape[2:]
    unit_decay = jnp.ones((channels,), jnp.float32)
    zero_state = jnp.zeros(state_shape, jnp.float32)
    cell_count = rgb_maps.shape[1] * lax.axis_size("tm") * rgb_maps.shape[2] * rgb_maps.shape[3]
    clip_total = rgb_maps.shape[0] * lax.axis_size("batch")
    in_rgb, part_rgb, total_rgb, end_rgb = local_states(rgb_maps, in_weights[0], decay[0])
    in_flow, part_flow, total_flow, end_flow = local_states(flow_maps, in_weights[1], decay[1])
    scanned = prefix(
        (total_rgb, end_rgb, total_flow, end_flow),
        "tm",
        compose_pair,
        (unit_decay, zero_state, unit_decay, zero_state),
        False,
    )
    income_rgb = scanned[1]
    income_flow = scanned[3]
    states_rgb, mixed_rgb, pooled_rgb = finish_states(
        in_rgb, part_rgb, decay[0], income_rgb, out_weights[0], skip[0]
    )
    states_flow, mixed_flow, pooled_flow = finish_states(
        in_flow, part_flow, decay[1], income_flow, out_weights[1], skip[1]
    )
    pooled_sums = lax.psum((pooled_rgb, pooled_flow), "tm")
    pooled_views = (pooled_sums[0] / cell_count, pooled_sums[1] / cell_count)
    hidden_views = [
        jnp.dot(
            pooled_views[view_idx], proj_in, precision=HIGHEST, preferred_element_type=jnp.float32
        )
        for view_idx in range(2)
    ]
    hidden_totals = lax.psum(
        (jnp.sum(hidden_views[0], axis=0), jnp.sum(hidden_views[1], axis=0)), "batch"
    )
    hidden_cent = [
        hidden_views[view_idx] - hidden_totals[view_idx] / clip_total for view_idx in range(2)
    ]
    hidden_squares = lax.psum(
        (
            jnp.sum(hidden_cent[0] * hidden_cent[0], axis=0),
            jnp.sum(hidden_cent[1] * hidden_cent[1], axis=0),
        ),
        "batch",
    )
    hidden_scale = [
        lax.rsqrt(hidden_squares[view_idx] / clip_total + EPSILON) for view_idx in range(2)
    ]
    hidden_x = [hidden_cent[view_idx] * hidden_scale[view_idx] for view_idx in range(2)]
    hidden_n = [hidden_x[view_idx] * proj_gain for view_idx in range(2)]
    z_views = [
        jnp.dot(
            jnp.maximum(hidden_n[view_idx], 0.0).astype(jnp.bfloat16),
            proj_out,
            preferred_element_type=jnp.float32,
        )
        for view_idx in range(2)
    ]
    z_totals = lax.psum((jnp.sum(z_views[0], axis=0), jnp.sum(z_views[1], axis=0)), "batch")
    z_cent = [z_views[view_idx] - z_totals[view_idx] / clip_total for view_idx in range(2)]
    z_squares = lax.psum(
        (jnp.sum(z_cent[0] * z_cent[0], axis=0), jnp.sum(z_cent[1] * z_cent[1], axis=0)), "batch"
    )
    z_scale = [lax.rsqrt(z_squares[view_idx] / clip_total + EPSILON) for view_idx in range(2)]
    z_x = [z_cent[view_idx] * z_scale[view_idx] for view_idx in range(2)]
    zn_rgb = z_x[0].astype(jnp.bfloat16)
    zn_flow = z_x[1].astype(jnp.bfloat16)
    proj_width = proj_out.shape[1]
    row_block = proj_width // lax.axis_size("tm")
    first_row = lax.axis_index("tm") * row_block
    own_block = lax.dynamic_slice_in_dim(zn_rgb, first_row, row_block, 1)
    gathered_block, gathered_flow = (
        lax.all_gather(own_block, "batch", axis=0, tiled=True),
        lax.all_gather(zn_flow, "batch", axis=0, tiled=True),
    )
    corr_block = (
        lax.dot_general(
            gathered_block,
            gathered_flow,
            (((0,), (0,)), ((), ())),
            preferred_element_type=jnp.float32,
        )
        / clip_total
    )
    grad_block = barlow_grads(corr_block, first_row)
    flow_wide = zn_flow.astype(jnp.float32)
    block_wide = own_block.astype(jnp.float32)
    dzn_cols = (
        lax.dot_general(flow_wide, grad_block, (((1,), (1,)), ((), ())), precision=HIGHEST)
        / clip_total
    )
    dzn_rgb = lax.all_gather(dzn_cols, "tm", axis=1, tiled=True)
    dzn_flow = lax.psum(jnp.dot(block_wide, grad_block, precision=HIGHEST) / clip_total, "tm")
    dzn_views = (dzn_rgb, dzn_flow)
    z_back = lax.psum(
        (
            jnp.sum(dzn_rgb, axis=0),
            jnp.sum(dzn_rgb * z_x[0], axis=0),
            jnp.sum(dzn_flow, axis=0),
            jnp.sum(dzn_flow * z_x[1], axis=0),
        ),
        "batch",
    )
    dxh_views = []
    for view_idx in range(2):
        dz_b = (
            (
                dzn_views[view_idx]
                - z_back[2 * view_idx] / clip_total
                - z_x[view_idx] * (z_back[2 * view_idx + 1] / clip_total)
            )
            * z_scale[view_idx]
        ).astype(jnp.bfloat16)
        drelu = lax.dot_general(
            dz_b, proj_out, (((1,), (1,)), ((), ())), preferred_element_type=jnp.float32
        )
        dxh_views.append(jnp.where(hidden_n[view_idx] > 0, drelu, 0.0) * proj_gain)
    h_back = lax.psum(
        (
            jnp.sum(dxh_views[0], axis=0),
            jnp.sum(dxh_views[0] * hidden_x[0], axis=0),
            jnp.sum(dxh_views[1], axis=0),
            jnp.sum(dxh_views[1] * hidden_x[1], axis=0),
        ),
        "batch",
    )
    dpooled = []
    for view_idx in range(2):
        dhidden = (
            dxh_views[view_idx]
            - h_back[2 * view_idx] / clip_total
            - hidden_x[view_idx] * (h_back[2 * view_idx + 1] / clip_total)
        ) * hidden_scale[view_idx]
        dpooled.append(
            lax.dot_general(dhidden, proj_in, (((1,), (1,)), ((), ())), precision=HIGHEST)
        )
    dmix_rgb, out_grad_rgb, adj_rgb, send_rgb = local_adjoint(
        dpooled[0], mixed_rgb, states_rgb, decay[0], out_weights[0], cell_count
    )
    dmix_flow, out_grad_flow, adj_flow, send_flow = local_adjoint(
        dpooled[1], mixed_flow, states_flow, decay[1], out_weights[1], cell_count
    )
    returned = prefix(
        (total_rgb, send_rgb, total_flow, send_flow),
        "tm",
        compose_pair,
        (unit_decay, zero_state, unit_decay, zero_state),
        True,
    )
    back_rgb = returned[1]
    back_flow = returned[3]
    in_grad_rgb = finish_adjoint(rgb_maps, dmix_rgb, adj_rgb, decay[0], back_rgb, skip[0])
    in_grad_flow = finish_adjoint(flow_maps, dmix_flow, adj_flow, decay[1], back_flow, skip[1])
    in_stack = jnp.stack([in_grad_rgb, in_grad_flow])
    out_stack = jnp.stack([out_grad_rgb, out_grad_flow])
    shares = (
        lax.psum_scatter(in_stack, "tm", scatter_dimension=1, tiled=True),
        lax.psum_scatter(out_stack, "tm", scatter_dimension=1, tiled=True),
    )
    share_sums = lax.psum((shares[0], shares[1]), "batch")
    whole = (
        lax.all_gather(share_sums[0], "tm", axis=1, tiled=True),
        lax.all_gather(share_sums[1], "tm", axis=1, tiled=True),
    )
    return (whole[0], whole[1])


def solution(mesh):
    return jax.shard_map(
        per_device,
        mesh=mesh,
        in_specs=(
            P("batch", "tm", None, None, None),
            P("batch", "tm", None, None, None),
            P(),
            P(),
            P(None, "tm", None),
            P(),
            P(),
            P(),
            P(),
        ),
        out_specs=(P(), P()),
        check_vma=False,
    )
```

profile of v0, /device:TPU:0, one launch (start us, length us, event | category | flops | bytes accessed | tf_op | source)
XLA Modules:
  0.0 675.8 jit_solution(4115800723898485168)
XLA Ops:
  9.7 2.3 fusion.25
  20.8 5.6 convolution_convert_fusion
  39.4 7.1 %fusion.79 = bf16[4,8,16,16,128]{4,3,2,0,1:T(8,128)(2,1)S(1)} fusion(bf16[4,8,16,16,1152]{4,3,2,1,0:T(8,128)(2,1)S(1)} %fusion.40, bf16[2,1152,128]{2,1,0:T(8,128)(2,1)} %param.15), kind=kOutput, calls=%fused_computation.152 | convolution fusion | flops 2416967680 | bytes 21266432 | tf_op jit(solution)/shard_map/dot_general | solution.py:45
  55.1 10.3 %all-gather.2 = f32[8,1,128]{2,1,0:T(1,128)S(1)} all-gather(f32[1,1,128]{2,1,0:T(1,128)S(1)} %bitcast.624), channel_id=2, replica_groups=mesh['tm'=8,'batch'=4] {'tm'}, dimensions={0}, use_global_device_ids=true | all-gather | bytes 4608 | tf_op jit(solution)/shard_map/all_gather | solution.py:13
  65.4 8.7 %all-gather.3 = f32[8,1,128]{2,1,0:T(1,128)S(1)} all-gather(f32[1,1,128]{2,1,0:T(1,128)S(1)} %bitcast.623), channel_id=3, replica_groups=mesh['tm'=8,'batch'=4] {'tm'}, dimensions={0}, use_global_device_ids=true | all-gather | bytes 4608 | tf_op jit(solution)/shard_map/all_gather | solution.py:13
  74.1 2.1 fusion.84
  77.1 2.0 fusion.157
  90.5 17.5 %all-gather.15.cloned.1.call-done = f32[8,4,16,16,128]{4,3,2,1,0:T(8,128)} async-done(((f32[1,4,16,16,128]{4,3,2,1,0:T(8,128)}), f32[8,4,16,16,128]{4,3,2,1,0:T(8,128)}) %all-gather.15.cloned.1.call-update) | async-done | bytes 4194320 | tf_op jit(solution)/shard_map/all_gather | solution.py:13
  108.0 21.1 %while.34 = (s32[]{:T(128)}, f32[4,16,16,128]{3,2,1,0:T(8,128)}, f32[4,16,16,128]{3,2,1,0:T(8,128)}, s32[]{:T(128)}, f32[8,128]{1,0:T(8,128)S(1)}, /*index=5*/f3...) while((s32[]{:T(128)}, f32[4,16,16,128]{3,2,1,0:T(8,128)}, ...), condition=%wide.region_4.5_spmd.clone, body=%wide.region_3.4_spmd.clone.sunk | while | flops 1048580 | bytes 3148933 | solution.py:24
  108.0 2.3 fusion.258
  110.3 2.6 fusion.258
  113.0 2.6 fusion.258
  115.7 2.6 fusion.258
  118.3 2.6 fusion.258
  121.0 2.6 fusion.258
  123.6 2.6 fusion.258
  126.3 2.6 fusion.258
  129.1 2.9 add_convert_fusion.3
  136.1 3.1 constant_dynamic-update-slice_fusion.5
  143.8 6.0 add_convert_fusion.2
  149.8 2.2 fusion.49
  152.0 1.9 fusion.50
  153.8 2.5 fusion.51
  156.4 2.3 fusion.52
  158.7 4.2 constant_dynamic-update-slice_fusion.9
  162.8 2.5 fusion.53
  165.3 2.3 fusion.54
  169.4 2.4 fusion.56
  171.8 10.9 %multiply_reduce_fusion.1 = (f32[4,128]{1,0:T(4,128)S(1)}, f32[4,8,16,16,128]{4,3,2,1,0:T(8,128)}) fusion(bf16[4,8,16,16,128]{4,3,2,1,0:T(8,128)(2,1)S(1)} %copy-done.9, f32[128]{0:T(128)S(1)} %get-tuple-element.504, bf16[2,1152,128]{2,1,0:T(8,128)(2,1)S(1)} %copy-done.22, bf16[4,8,16,16,1152]{4,3,2,0,1:T(8,128)(2,1)} %copy-done.26), kind=kOutput, calls=%fused_computation.83 | convolution fusion | flops 2424307200 | bytes 25463296 | tf_op jit(solution)/shard_map/dot_general | solution.py:45
  182.7 11.8 %multiply_reduce_fusion = (f32[4,128]{1,0:T(4,128)S(1)}, f32[4,8,16,16,128]{4,3,2,0,1:T(8,128)}, f32[4,8,16,16,128]{4,3,2,0,1:T(8,128)}) fusion(bf16[4,8,16,16,128]{4,3,2,0,1:T(8,128)(2,1)S(1)} %copy-done.13, f32[128]{0:T(128)S(1)} %get-tuple-element.505, bf16[4,8,16,16,1152]{4,3,2,0,1:T(8,128)(2,1)} %fusion.56, bf16[2,1152,128]{2,1,0:T(8,128)(2,1)S(1)} %copy-done.22), kind=kOutput, calls=%fused_computation.79 | convolution fusion | flops 2426404352 | bytes 29657600 | tf_op jit(solution)/shard_map/dot_general | solution.py:45
  194.5 13.1 %all-reduce.8 = (f32[4,128]{1,0:T(4,128)S(1)}, f32[4,128]{1,0:T(4,128)S(1)}) all-reduce(f32[4,128]{1,0:T(4,128)S(1)} %get-tuple-element.506, f32[4,128]{1,0:T(4,128)S(1)} %get-tuple-element.477), channel_id=1, replica_groups=mesh['tm'=8,'batch'=4] {'tm'}, use_global_device_ids=true, to_apply=%region_6.7 | all-reduce | flops 1024 | bytes 8192 | tf_op jit(solution)/shard_map/psum | solution.py:158
  208.8 18.7 %all-reduce.14 = (f32[2048]{0:T(1024)S(1)}, f32[2048]{0:T(1024)S(1)}) all-reduce(f32[2048]{0:T(1024)S(1)} %get-tuple-element.508, f32[2048]{0:T(1024)S(1)} %get-tuple-element.510), channel_id=1, replica_groups=mesh['tm'=8,'batch'=4] {'batch'}, use_global_device_ids=true, to_apply=%region_8.9 | all-reduce | flops 4096 | bytes 32768 | tf_op jit(solution)/shard_map/psum | solution.py:166
  227.6 16.0 %all-reduce.13 = (f32[2048]{0:T(1024)S(1)}, f32[2048]{0:T(1024)S(1)}) all-reduce(f32[2048]{0:T(1024)S(1)} %multiply_reduce_fusion.9, f32[2048]{0:T(1024)S(1)} %multiply_reduce_fusion.8), channel_id=1, replica_groups=mesh['tm'=8,'batch'=4] {'batch'}, use_global_device_ids=true, to_apply=%region_10.11 | all-reduce | flops 4096 | bytes 32768 | tf_op jit(solution)/shard_map/psum | solution.py:172
  243.6 4.6 fusion.225
  248.2 4.6 fusion.224
  252.8 16.4 %all-reduce.12 = (f32[2048]{0:T(1024)S(1)}, f32[2048]{0:T(1024)S(1)}) all-reduce(f32[2048]{0:T(1024)S(1)} %get-tuple-element.512, f32[2048]{0:T(1024)S(1)} %get-tuple-element.514), channel_id=1, replica_groups=mesh['tm'=8,'batch'=4] {'batch'}, use_global_device_ids=true, to_apply=%region_23.24 | all-reduce | flops 4096 | bytes 32768 | tf_op jit(solution)/shard_map/psum | solution.py:192
  269.3 15.6 %all-reduce.11 = (f32[2048]{0:T(1024)S(1)}, f32[2048]{0:T(1024)S(1)}) all-reduce(f32[2048]{0:T(1024)S(1)} %multiply_reduce_fusion.6, f32[2048]{0:T(1024)S(1)} %multiply_reduce_fusion.7), channel_id=1, replica_groups=mesh['tm'=8,'batch'=4] {'batch'}, use_global_device_ids=true, to_apply=%region_25.26 | all-reduce | flops 4096 | bytes 32768 | tf_op jit(solution)/shard_map/psum | solution.py:194
  284.9 13.1 %all-gather.5 = bf16[4,4,2048]{2,1,0:T(4,128)(2,1)S(1)} all-gather(bf16[1,4,2048]{2,1,0:T(4,128)(2,1)S(1)} %fusion.210), channel_id=1, replica_groups=mesh['tm'=8,'batch'=4] {'batch'}, dimensions={0}, use_global_device_ids=true | all-gather | bytes 81920 | tf_op jit(solution)/shard_map/all_gather | solution.py:207
  298.1 11.9 %all-gather.4 = bf16[4,4,256]{2,1,0:T(4,128)(2,1)S(1)} all-gather(bf16[1,4,256]{2,1,0:T(4,128)(2,1)S(1)} %fusion.202), channel_id=1, replica_groups=mesh['tm'=8,'batch'=4] {'batch'}, dimensions={0}, use_global_device_ids=true | all-gather | bytes 10240 | tf_op jit(solution)/shard_map/all_gather | solution.py:206
  312.5 9.0 %all_gather.55 = f32[4,2048]{1,0:T(4,128)S(1)} all-gather(f32[4,256]{1,0:T(4,128)S(1)} %convolution_multiply_fusion.1), channel_id=1, replica_groups=mesh['tm'=8,'batch'=4] {'tm'}, dimensions={1}, use_global_device_ids=true | all-gather | bytes 36864 | tf_op jit(solution)/shard_map/all_gather | solution.py:225
  321.6 23.6 %psum.161 = f32[4,2048]{1,0:T(4,128)S(1)} all-reduce(f32[4,2048]{1,0:T(4,128)S(1)} %convolution_multiply_fusion), channel_id=1, replica_groups=mesh['tm'=8,'batch'=4] {'tm'}, use_global_device_ids=true, to_apply=%region_35.36 | all-reduce | flops 8192 | bytes 65536 | tf_op jit(solution)/shard_map/psum | solution.py:226
  345.2 15.8 %all-reduce.10 = (f32[2048]{0:T(1024)S(1)}, f32[2048]{0:T(1024)S(1)}, f32[2048]{0:T(1024)S(1)}, f32[2048]{0:T(1024)S(1)}) all-reduce(f32[2048]{0:T(1024)S(1)} %get-tuple-element.406, f32[2048]{0:T(1024)S(1)} %get-tuple-element.405, f32[2048]{0:T(1024)S(1)} %get-tuple-element.402, ...), channel_id=1, replica_groups=mesh['tm'=8,'batch'=4] {'batch'}, use_global_device_ids=true, to_apply=%region_39.40 | all-reduce | flops 8192 | bytes 65536 | tf_op jit(solution)/shard_map/psum | solution.py:228
  361.1 5.7 fusion.214
  366.8 5.7 fusion.216
  372.4 17.8 %all-reduce.9 = (f32[2048]{0:T(1024)S(1)}, f32[2048]{0:T(1024)S(1)}, f32[2048]{0:T(1024)S(1)}, f32[2048]{0:T(1024)S(1)}) all-reduce(f32[2048]{0:T(1024)S(1)} %get-tuple-element.404, f32[2048]{0:T(1024)S(1)} %get-tuple-element.403, f32[2048]{0:T(1024)S(1)} %get-tuple-element.400, ...), channel_id=1, replica_groups=mesh['tm'=8,'batch'=4] {'batch'}, use_global_device_ids=true, to_apply=%region_43.44 | all-reduce | flops 8192 | bytes 65536 | tf_op jit(solution)/shard_map/psum | solution.py:251
  391.2 4.7 fusion.213
  405.3 5.5 fusion.226
  410.8 1.9 copy-done.6
  414.9 4.7 fusion.83
  428.7 5.3 fusion.227
  437.3 1.9 copy-done.27
  439.3 1.9 copy-done.28
  442.4 9.5 %fusion.17 = f32[1,1152,128]{2,1,0:T(8,128)S(1)} fusion(bf16[4,8,16,16,128]{4,3,2,1,0:T(8,128)(2,1)S(1)} %fusion.213, bf16[4,8,16,16,1152]{4,3,2,0,1:T(8,128)(2,1)} %copy-done.26), kind=kOutput, calls=%fused_computation.87 | convolution fusion | flops 2415919104 | bytes 21561344 | tf_op jit(solution)/shard_map/dot_general | solution.py:57
  451.9 9.6 %fusion.20 = f32[1,1152,128]{2,1,0:T(8,128)S(1)} fusion(bf16[4,8,16,16,128]{4,3,2,1,0:T(8,128)(2,1)S(1)} %copy-done.3, bf16[4,8,16,16,1152]{4,3,2,0,1:T(8,128)(2,1)} %fusion.56), kind=kOutput, calls=%fused_computation.88 | convolution fusion | flops 2415919104 | bytes 21561344 | tf_op jit(solution)/shard_map/dot_general | solution.py:57
  463.0 22.6 %all-gather.19.cloned.1.call-done = f32[8,4,16,16,128]{4,3,2,1,0:T(8,128)} async-done(((f32[1,4,16,16,128]{4,3,2,1,0:T(8,128)}), f32[8,4,16,16,128]{4,3,2,1,0:T(8,128)}) %all-gather.19.cloned.1.call-update) | async-done | bytes 4194320 | tf_op jit(solution)/shard_map/all_gather | solution.py:13
  485.6 24.4 %while.35 = (s32[]{:T(128)}, f32[4,16,16,128]{3,2,1,0:T(8,128)S(1)}, f32[4,16,16,128]{3,2,1,0:T(8,128)S(1)}, s32[]{:T(128)}, f32[8,128]{1,0:T(8,128)}, /*index=5...) while((s32[]{:T(128)}, ...), condition=%wide.region_45.46_spmd.clone, body=%wide.region_44.45_spmd.clone.sunk | while | flops 1048584 | bytes 3148995 | solution.py:24
  510.1 14.4 %convolution_bitcast_fusion.1 = f32[1,1152,128]{2,1,0:T(8,128)S(1)} fusion(bf16[4,8,16,16,1152]{4,3,2,1,0:T(8,128)(2,1)} %copy-done.24, f32[4,8,16,16,128]{4,3,2,1,0:T(8,128)} %copy-done.27, f32[4,16,16,128]{3,2,1,0:T(8,128)S(1)} %get-tuple-element.343, f32[8,128]{1,0:T(8,128)S(1)} %copy-done.37, f32[128]{0:T(128)S(1)} %copy-done.39, ...), kind=kOutput, calls=%fused_computation.90 | convolution fusion | flops 2432696320 | bytes 30480896 | tf_op jit(solution)/shard_map/dot_general | solution.py:57
  524.5 11.4 %convolution_bitcast_fusion = f32[1,1152,128]{2,1,0:T(8,128)S(1)} fusion(bf16[4,8,16,16,1152]{4,3,2,1,0:T(8,128)(2,1)} %copy-done.25, f32[4,8,16,16,128]{4,3,2,1,0:T(8,128)} %copy-done.28, f32[128]{0:T(128)S(1)} %copy-done.44, f32[4,16,16,128]{3,2,1,0:T(8,128)S(1)} %get-tuple-element.344, f32[8,128]{1,0:T(8,128)S(1)} %copy-done.36, ...), kind=kOutput, calls=%fused_computation.89 | convolution fusion | flops 2424307712 | bytes 32578048 | tf_op jit(solution)/shard_map/dot_general | solution.py:57
  537.1 37.0 %reduce-scatter.3.cloned.1.call-done = f32[2,144,128]{2,1,0:T(8,128)} async-done(((f32[2,1152,128]{2,1,0:T(8,128)}), f32[2,144,128]{2,1,0:T(8,128)}) %reduce-scatter.3.cloned.1.call-update) | async-done | bytes 147472 | tf_op jit(solution)/shard_map/reduce_scatter | solution.py:290
  574.2 38.4 %all-reduce.18.cloned.1.call-done = (f32[2,144,128]{2,1,0:T(8,128)}, f32[2,144,128]{2,1,0:T(8,128)}) async-done(((f32[2,144,128]{2,1,0:T(8,128)}, f32[2,144,128]{2,1,0:T(8,128)}), (f32[2,144,128]{2,1,0:T(8,128)}, f32[2,144,128]{2,1,0:T(8,128)})) %all-reduce.18.cloned.1.call-update) | async-done | bytes 294928 | tf_op jit(solution)/shard_map/psum | solution.py:293
  613.3 25.0 %all-gather.21.cloned.1.call-done = f32[2,1152,128]{2,1,0:T(8,128)} async-done(((f32[2,144,128]{2,1,0:T(8,128)}), f32[2,1152,128]{2,1,0:T(8,128)}) %all-gather.21.cloned.1.call-update) | async-done | bytes 1179664 | tf_op jit(solution)/shard_map/all_gather | solution.py:295
  638.3 26.0 %all-gather.23.cloned.1.call-done = f32[2,1152,128]{2,1,0:T(8,128)} async-done(((f32[2,144,128]{2,1,0:T(8,128)}), f32[2,1152,128]{2,1,0:T(8,128)}) %all-gather.23.cloned.1.call-update) | async-done | bytes 1179664 | tf_op jit(solution)/shard_map/all_gather | solution.py:296
  664.3 2.4 copy.296
  666.7 2.4 copy.297
  (285 shorter events, 113.0 us)
Async XLA Ops:
  7.2 200.4 %copy-start = (f32[128,2048]{1,0:T(8,128)S(1)}, f32[128,2048]{1,0:T(8,128)}, u32[]{:S(2)}) copy-start(f32[128,2048]{1,0:T(8,128)} %param.19) | copy-start | bytes 3145732
  7.2 4.8 copy-start.4
  7.2 83.3 %all-gather.13.cloned.1.call-start = ((), (), s32[]{:S(2)}) async-start(), calls=%async_computation.2 | async-start | bytes 4718592 | tf_op jit(solution)/shard_map/all_gather | solution.py:13
  9.7 17.5 %copy-start.30 = (f32[128]{0:T(128)}, f32[128]{0:T(128)S(1)}, u32[]{:S(2)}) copy-start(f32[128]{0:T(128)S(1)} %get-tuple-element.489) | copy-start | bytes 1540
  18.7 2.1 copy-start.45
  20.8 6.4 copy-start.24
  27.2 1.3 copy-start.8
  27.2 2.6 copy-start.5
  29.8 78.2 %all-gather.15.cloned.1.call-start = ((), (), s32[]{:S(2)}) async-start(), calls=%async_computation.3 | async-start | bytes 4718592 | tf_op jit(solution)/shard_map/all_gather | solution.py:13
  39.3 7.1 %copy-start.25 = (bf16[4,8,16,16,1152]{4,3,2,1,0:T(8,128)(2,1)}, bf16[4,8,16,16,1152]{4,3,2,1,0:T(8,128)(2,1)S(1)}, u32[]{:S(2)}) copy-start(bf16[4,8,16,16,1152]{4,3,2,1,0:T(8,128)(2,1)S(1)} %fusion.40) | copy-start | bytes 56623108
  39.3 9.8 %copy-start.29 = (f32[2,8,128]{2,1,0:T(8,128)S(1)}, f32[2,8,128]{2,1,0:T(8,128)}, u32[]{:S(2)}) copy-start(f32[2,8,128]{2,1,0:T(8,128)} %param.17) | copy-start | bytes 24580
  46.4 1.4 copy-start.11
  46.4 27.6 %copy-start.9 = (bf16[4,8,16,16,128]{4,3,2,1,0:T(8,128)(2,1)S(1)}, bf16[4,8,16,16,128]{4,3,2,1,0:T(8,128)(2,1)}, u32[]{:S(2)}) copy-start(bf16[4,8,16,16,128]{4,3,2,1,0:T(8,128)(2,1)} %copy-done.8) | copy-start | bytes 6291460
  46.5 27.6 %copy-start.42 = (f32[2,128]{1,0:T(2,128)S(1)}, f32[2,128]{1,0:T(2,128)}, u32[]{:S(2)}) copy-start(f32[2,128]{1,0:T(2,128)} %param.18) | copy-start | bytes 3076
  49.0 414.0 %all-gather.17.cloned.1.call-start = ((), (), s32[]{:S(2)}) async-start(), calls=%async_computation.4 | async-start | bytes 4718592 | tf_op jit(solution)/shard_map/all_gather | solution.py:13
  55.1 24.9 %copy-start.12 = (bf16[4,8,16,16,128]{4,3,2,0,1:T(8,128)(2,1)S(1)}, bf16[4,8,16,16,128]{4,3,2,0,1:T(8,128)(2,1)}, u32[]{:S(2)}) copy-start(bf16[4,8,16,16,128]{4,3,2,0,1:T(8,128)(2,1)} %copy-done.11) | copy-start | bytes 6291460
  74.1 97.7 %copy-start.38 = (f32[128]{0:T(128)}, f32[128]{0:T(128)S(1)}, u32[]{:S(2)}) copy-start(f32[128]{0:T(128)S(1)} %get-tuple-element.504) | copy-start | bytes 1540
  74.1 108.6 %copy-start.43 = (f32[128]{0:T(128)}, f32[128]{0:T(128)S(1)}, u32[]{:S(2)}) copy-start(f32[128]{0:T(128)S(1)} %get-tuple-element.505) | copy-start | bytes 1540
  84.0 4.6 copy-start.31
  129.1 3.7 copy-start.34
  129.1 3.7 copy-start.35
  133.7 2.5 copy-start.14
  141.7 2.1 copy-start.15
  143.8 19.1 %copy-start.26 = (bf16[4,8,16,16,1152]{4,3,2,0,1:T(8,128)(2,1)}, bf16[4,8,16,16,1152]{4,3,2,0,1:T(8,128)(2,1)S(1)}, u32[]{:S(2)}) copy-start(bf16[4,8,16,16,1152]{4,3,2,0,1:T(8,128)(2,1)S(1)} %fusion.48) | copy-start | bytes 56623108
  167.6 4.2 copy-start.22
  171.8 10.9 %copy-start.13 = (bf16[4,8,16,16,128]{4,3,2,0,1:T(8,128)(2,1)S(1)}, bf16[4,8,16,16,128]{4,3,2,0,1:T(8,128)(2,1)}, u32[]{:S(2)}) copy-start(bf16[4,8,16,16,128]{4,3,2,0,1:T(8,128)(2,1)} %copy-done.11) | copy-start | bytes 6291460
  182.7 60.9 %copy-start.23 = (f32[2048]{0:T(1024)S(1)}, f32[2048]{0:T(1024)}, u32[]{:S(2)}) copy-start(f32[2048]{0:T(1024)} %param.20) | copy-start | bytes 24580
  366.7 24.4 %copy-start.39 = (f32[128]{0:T(128)S(1)}, f32[128]{0:T(128)}, u32[]{:S(2)}) copy-start(f32[128]{0:T(128)} %copy-done.38) | copy-start | bytes 1540
  403.3 2.0 copy-start.21
  405.3 7.5 %copy-start.41 = (f32[128]{0:T(128)S(1)}, f32[128]{0:T(128)}, u32[]{:S(2)}) copy-start(f32[128]{0:T(128)} %get-tuple-element.496) | copy-start | bytes 1540
  410.8 1.9 copy-start.6
  413.9 71.7 %all-gather.19.cloned.1.call-start = ((), (), s32[]{:S(2)}) async-start(), calls=%async_computation.5 | async-start | bytes 4718592 | tf_op jit(solution)/shard_map/all_gather | solution.py:13
  414.9 4.7 copy-start.32
  419.5 8.0 %copy-start.2 = (bf16[4,8,16,16,128]{4,3,2,1,0:T(8,128)(2,1)}, bf16[4,8,16,16,128]{4,3,2,1,0:T(8,128)(2,1)S(1)}, u32[]{:S(2)}) copy-start(bf16[4,8,16,16,128]{4,3,2,1,0:T(8,128)(2,1)S(1)} %fusion.83) | copy-start | bytes 6291460
  426.8 1.9 copy-start.20
  434.3 2.2 copy-start.7
  436.9 4.4 copy-start.40
  437.3 2.0 copy-start.27
  439.3 1.9 copy-start.28
  442.4 94.7 %reduce-scatter.5.cloned.1.call-start = ((), (), s32[]{:S(2)}) async-start(), calls=%async_computation.8 | async-start | bytes 1327104 | tf_op jit(solution)/shard_map/reduce_scatter | solution.py:291
  442.4 9.5 %copy-start.3 = (bf16[4,8,16,16,128]{4,3,2,1,0:T(8,128)(2,1)S(1)}, bf16[4,8,16,16,128]{4,3,2,1,0:T(8,128)(2,1)}, u32[]{:S(2)}) copy-start(bf16[4,8,16,16,128]{4,3,2,1,0:T(8,128)(2,1)} %copy-done.2) | copy-start | bytes 6291460
  451.9 33.7 %copy-start.16 = (f32[4,16,16,128]{3,2,1,0:T(8,128)S(1)}, f32[4,16,16,128]{3,2,1,0:T(8,128)}, u32[]{:S(2)}) copy-start(f32[4,16,16,128]{3,2,1,0:T(8,128)} %custom-call.2) | copy-start | bytes 1572868
  451.9 33.7 %copy-start.17 = (f32[4,16,16,128]{3,2,1,0:T(8,128)S(1)}, f32[4,16,16,128]{3,2,1,0:T(8,128)}, u32[]{:S(2)}) copy-start(f32[4,16,16,128]{3,2,1,0:T(8,128)} %custom-call.3) | copy-start | bytes 1572868
  462.7 111.4 %reduce-scatter.3.cloned.1.call-start = ((), (), s32[]{:S(2)}) async-start(), calls=%async_computation.6 | async-start | bytes 1327104 | tf_op jit(solution)/shard_map/reduce_scatter | solution.py:290
  485.6 24.4 %copy-start.10 = (bf16[4,8,16,16,128]{4,3,2,1,0:T(8,128)(2,1)S(1)}, bf16[4,8,16,16,128]{4,3,2,1,0:T(8,128)(2,1)}, u32[]{:S(2)}) copy-start(bf16[4,8,16,16,128]{4,3,2,1,0:T(8,128)(2,1)} %copy-done.8) | copy-start | bytes 6291460
  485.6 24.4 %copy-start.37 = (f32[8,128]{1,0:T(8,128)S(1)}, f32[8,128]{1,0:T(8,128)}, u32[]{:S(2)}) copy-start(f32[8,128]{1,0:T(8,128)} %concatenate.33) | copy-start | bytes 12292
  510.0 14.4 %copy-start.18 = (f32[4,8,16,16,128]{4,3,2,0,1:T(8,128)S(1)}, f32[4,8,16,16,128]{4,3,2,0,1:T(8,128)}, u32[]{:S(2)}) copy-start(f32[4,8,16,16,128]{4,3,2,0,1:T(8,128)} %get-tuple-element.478) | copy-start | bytes 12582916
  510.0 14.4 %copy-start.19 = (f32[4,8,16,16,128]{4,3,2,0,1:T(8,128)S(1)}, f32[4,8,16,16,128]{4,3,2,0,1:T(8,128)}, u32[]{:S(2)}) copy-start(f32[4,8,16,16,128]{4,3,2,0,1:T(8,128)} %get-tuple-element.479) | copy-start | bytes 12582916
  510.0 14.4 %copy-start.33 = (f32[4,128]{1,0:T(4,128)S(1)}, f32[4,128]{1,0:T(4,128)}, u32[]{:S(2)}) copy-start(f32[4,128]{1,0:T(4,128)} %copy-done.32) | copy-start | bytes 6148
  510.1 14.4 %copy-start.36 = (f32[8,128]{1,0:T(8,128)S(1)}, f32[8,128]{1,0:T(8,128)}, u32[]{:S(2)}) copy-start(f32[8,128]{1,0:T(8,128)} %concatenate.35) | copy-start | bytes 12292
  510.1 14.4 %copy-start.44 = (f32[128]{0:T(128)S(1)}, f32[128]{0:T(128)}, u32[]{:S(2)}) copy-start(f32[128]{0:T(128)} %copy-done.43) | copy-start | bytes 1540
  524.5 144.6 %copy-start.1 = (f32[128,2048]{1,0:T(8,128)S(1)}, f32[128,2048]{1,0:T(8,128)}, u32[]{:S(2)}) copy-start(f32[128,2048]{1,0:T(8,128)} %param.19) | copy-start | bytes 3145732
  537.0 75.5 %all-reduce.18.cloned.1.call-start = ((), (), s32[]{:S(2)}) async-start(), calls=%async_computation.10 | async-start | bytes 589824 | tf_op jit(solution)/shard_map/psum | solution.py:293
  574.1 64.2 %all-gather.21.cloned.1.call-start = ((), (), s32[]{:S(2)}) async-start(), calls=%async_computation.7 | async-start | bytes 1327104 | tf_op jit(solution)/shard_map/all_gather | solution.py:295
  612.6 51.7 %all-gather.23.cloned.1.call-start = ((), (), s32[]{:S(2)}) async-start(), calls=%async_computation.9 | async-start | bytes 1327104 | tf_op jit(solution)/shard_map/all_gather | solution.py:296
Sparse Core Ops, SparseCore 0:
  29.9 39.4 all-gather.12
  71.2 36.7 all-gather.14
  414.0 33.0 all-gather.16
  448.8 36.7 all-gather.18
  489.2 36.7 reduce-scatter.4
  537.1 36.8 reduce-scatter.2
  576.5 36.0 all-reduce.17
  614.5 23.8 all-gather.20
  640.2 24.0 all-gather.22
where the time goes:
time: 685 us; the launch traced here: 676 us
  blocking collectives  190 us (28%)
  waiting for transfers between devices  167 us (24%)
  matrix products  117 us (17%)
  local copies, waits for them, and re-layouts  100 us (15%)
  other arithmetic  85 us (12%)
  between operations  15.3 us (2%)
    unnamed x149, local copies, waits for them, and re-layouts  73 us
    dot_general x6, matrix products, convolve(): result = jnp.dot(flat, weights, preferred_element_type=jnp.float32)  46.1 us
    dot_general x4, matrix products, weight_product(): lax.dot_general(flat, grads.reshape(-1, grads.shape[-1]), (((0,), (0,)),...  44.9 us
    all_gather x4, waiting for transfers between devices, prefix(): everything = jax.tree.map(lambda part: lax.all_gather(part, axis), x)  40.1 us
    psum x1, waiting for transfers between devices, per_device(): share_sums = lax.psum((shares[0], shares[1]), 'batch')  38.4 us
    reduce_scatter x1, waiting for transfers between devices, per_device(): lax.psum_scatter(in_stack, 'tm', scatter_dimension=1, tiled=True)  37 us
    select_n x16, other arithmetic, lap(): return jax.tree.map(lambda a, b: jnp.where(reached, a, b), new, before)  33.9 us
    all_gather x1, waiting for transfers between devices, per_device(): lax.all_gather(share_sums[1], 'tm', axis=1, tiled=True)  26 us
  transfers between devices with their start and end apart: 9, of which 6 were waited for; matrix products, arithmetic and copies ran while one was open for 20% of the time, Pallas kernels for 0%

commit v1 on v0

--- a/solution.py
+++ b/solution.py
@@ -1,6 +1,10 @@
+import functools
+
 import jax
 import jax.numpy as jnp
 from jax import lax
+from jax.experimental import pallas as pl
+from jax.experimental.pallas import tpu as pltpu
 from jax.sharding import PartitionSpec as P
 
 LAMBDA_OFF = 0.0051
@@ -129,7 +133,7 @@
     return jnp.where(eye_mask, -2.0 * (1.0 - corr_rows), 2.0 * LAMBDA_OFF * corr_rows)
 
 
-def per_device(
+def scanned_per_device(
     rgb_maps, flow_maps, in_weights, out_weights, decay, skip, proj_in, proj_gain, proj_out
 ):
     channels = rgb_maps.shape[-1]
@@ -298,6 +302,555 @@
     return (whole[0], whole[1])
 
 
+BLOCK = 8
+VMEM_BYTES = 56 * 1024 * 1024
+
+
+MESH = pl.DeviceIdType.MESH
+
+
+def greet(places):
+    barrier = pltpu.get_barrier_semaphore()
+    for place in places:
+        pl.semaphore_signal(barrier, inc=1, device_id=place, device_id_type=MESH)
+    pl.semaphore_wait(barrier, len(places))
+
+
+def exchange_kernel(rgb, flow, decay, maps, decays, send, recv, send_decay, recv_decay, own):
+    me, peers = (lax.axis_index("tm"), lax.axis_size("tm"))
+    clips, frames = rgb.shape[:2]
+    here = pl.ds(pl.multiple_of(me * frames, frames), frames)
+    others = [lax.rem(me + k, peers) for k in range(1, peers)]
+    greet([{"tm": other} for other in others])
+    for view, source in enumerate((rgb, flow)):
+
+        @pl.when(me // clips == view)
+        def _(source=source):
+            pltpu.make_async_copy(source.at[lax.rem(me, clips)], maps.at[here], own.at[0]).start()
+
+    kept = pltpu.make_async_copy(decay.at[me // clips], decays.at[here], own.at[1])
+    kept.start()
+    copies = []
+    for k, other in enumerate(others):
+        for view, source in enumerate((rgb, flow)):
+            copy = pltpu.make_async_remote_copy(
+                src_ref=source.at[lax.rem(other, clips)],
+                dst_ref=maps.at[here],
+                send_sem=send.at[k],
+                recv_sem=recv.at[k],
+                device_id={"tm": other},
+                device_id_type=MESH,
+            )
+
+            @pl.when(other // clips == view)
+            def _(copy=copy):
+                copy.start()
+
+        copies.append(copy)
+        small = pltpu.make_async_remote_copy(
+            src_ref=decay.at[other // clips],
+            dst_ref=decays.at[here],
+            send_sem=send_decay.at[k],
+            recv_sem=recv_decay.at[k],
+            device_id={"tm": other},
+            device_id_type=MESH,
+        )
+        small.start()
+        copies.append(small)
+    for copy in copies:
+        copy.wait()
+    pltpu.make_async_copy(rgb.at[0], maps.at[here], own.at[0]).wait()
+    kept.wait()
+
+
+def exchange(rgb_maps, flow_maps, decay):
+    clips, frames = rgb_maps.shape[:2]
+    peers = lax.axis_size("tm")
+    channels = decay.shape[-1]
+    others = pltpu.SemaphoreType.DMA((peers - 1,))
+    return pl.pallas_call(
+        exchange_kernel,
+        in_specs=[pl.BlockSpec(memory_space=pl.ANY)] * 3,
+        out_specs=[pl.BlockSpec(memory_space=pl.ANY)] * 2,
+        out_shape=[
+            jax.ShapeDtypeStruct((frames * peers,) + rgb_maps.shape[2:], rgb_maps.dtype),
+            jax.ShapeDtypeStruct((frames * peers, channels), decay.dtype),
+        ],
+        scratch_shapes=[others, others, others, others, pltpu.SemaphoreType.DMA((2,))],
+        compiler_params=pltpu.CompilerParams(collective_id=0, has_side_effects=True),
+    )(rgb_maps, flow_maps, decay)
+
+
+def gather_kernel(pooled, everyone, send, recv):
+    me, peers = (lax.axis_index("tm"), lax.axis_size("tm"))
+    ring, rings = (lax.axis_index("batch"), lax.axis_size("batch"))
+    near = [{"tm": lax.rem(me + k, peers)} for k in range(1, peers)]
+    far = [{"batch": lax.rem(ring + k, rings)} for k in range(1, rings)]
+    greet(near + far)
+    everyone[ring, me] = pooled[...]
+    copies = []
+    for wave, part in ((near, everyone.at[ring, me]), (far, everyone.at[ring])):
+        started = []
+        for place in wave:
+            at = len(copies) + len(started)
+            copy = pltpu.make_async_remote_copy(
+                src_ref=part,
+                dst_ref=part,
+                send_sem=send.at[at],
+                recv_sem=recv.at[at],
+                device_id=place,
+                device_id_type=MESH,
+            )
+            copy.start()
+            started.append(copy)
+        for copy in started:
+            copy.wait_recv()
+        copies += started
+    for copy in copies:
+        copy.wait_send()
+
+
+def gather(pooled):
+    peers, rings = (lax.axis_size("tm"), lax.axis_size("batch"))
+    count = pltpu.SemaphoreType.DMA((peers + rings - 2,))
+    return pl.pallas_call(
+        gather_kernel,
+        in_specs=[pl.BlockSpec(memory_space=pltpu.VMEM)],
+        out_specs=pl.BlockSpec(memory_space=pltpu.VMEM),
+        out_shape=jax.ShapeDtypeStruct((rings, peers) + pooled.shape, pooled.dtype),
+        scratch_shapes=[count, count],
+        compiler_params=pltpu.CompilerParams(collective_id=1, has_side_effects=True),
+    )(pooled)
+
+
+def reduce_kernel(grads, whole, from_core, to_x, from_x, acc, from_ring, send, recv):
+    me, ring, rings = (lax.axis_index("tm"), lax.axis_index("batch"), lax.axis_size("batch"))
+    core, x, y = (lax.rem(me, 2), lax.rem(me // 2, 2), me // 4)
+    sibling, across, beyond = (
+        {"tm": me + 1 - 2 * core},
+        {"tm": me + 2 - 4 * x},
+        {"tm": me + 4 - 8 * y},
+    )
+    others = [lax.rem(ring + k, rings) for k in range(1, rings)]
+    greet([sibling, across, beyond] + [{"batch": other} for other in others])
+    started = []
+
+    def push(source, target, place):
+        at = len(started)
+        copy = pltpu.make_async_remote_copy(
+            src_ref=source,
+            dst_ref=target,
+            send_sem=send.at[at],
+            recv_sem=recv.at[at],
+            device_id=place,
+            device_id_type=MESH,
+        )
+        copy.start()
+        started.append(copy)
+        return copy
+
+    passed = push(grads.at[1 - core, 1 - x], from_core.at[0], sibling)
+    kept = push(grads.at[1 - core, x], from_core.at[1], sibling)
+    passed.wait_recv()
+    to_x[...] = grads[core, 1 - x] + from_core[0]
+    crossed = push(to_x, from_x, across)
+    kept.wait_recv()
+    acc[...] = grads[core, x] + from_core[1]
+    crossed.wait_recv()
+    acc[...] += from_x[...]
+    arrivals = [
+        push(acc.at[other], from_ring.at[k], {"batch": other}) for k, other in enumerate(others)
+    ]
+    total = acc[ring]
+    for k, copy in enumerate(arrivals):
+        copy.wait_recv()
+        total = total + from_ring[k]
+    whole[y, core, x, ring] = total.astype(whole.dtype)
+    part = whole.at[y, core, x, ring]
+    for copy in [push(part, part, {"batch": other}) for other in others]:
+        copy.wait_recv()
+
+    def hand(at_y, at_x, place):
+        part = whole.at[at_y, core, at_x]
+        return push(part, part, place)
+
+    sideways, upward, inward = (hand(y, x, across), hand(y, x, beyond), [hand(y, x, sibling)])
+    sideways.wait_recv()
+    corner = hand(y, 1 - x, beyond)
+    inward.append(hand(y, 1 - x, sibling))
+    upward.wait_recv()
+    inward.append(hand(1 - y, x, sibling))
+    corner.wait_recv()
+    inward.append(hand(1 - y, 1 - x, sibling))
+    for copy in inward:
+        copy.wait_recv()
+    for copy in started:
+        copy.wait_send()
+
+
+def reduce_grads(grads):
+    rings = lax.axis_size("batch")
+    rows, channels = grads.shape
+    part = (rings, rows // (4 * rings), channels)
+    count = pltpu.SemaphoreType.DMA((3 + 2 * (rings - 1) + 7,))
+    return pl.pallas_call(
+        reduce_kernel,
+        in_specs=[pl.BlockSpec(memory_space=pltpu.VMEM)],
+        out_specs=pl.BlockSpec(memory_space=pltpu.VMEM),
+        out_shape=jax.ShapeDtypeStruct((2, 2, 2) + part, jnp.bfloat16),
+        scratch_shapes=[
+            pltpu.VMEM((2,) + part, jnp.float32),
+            pltpu.VMEM(part, jnp.float32),
+            pltpu.VMEM(part, jnp.float32),
+            pltpu.VMEM(part, jnp.float32),
+            pltpu.VMEM((rings - 1,) + part[1:], jnp.float32),
+            count,
+            count,
+        ],
+        compiler_params=pltpu.CompilerParams(
+            collective_id=2, has_side_effects=True, vmem_limit_bytes=VMEM_BYTES
+        ),
+    )(grads.reshape((2, 2) + part))
+
+
+def pair_weights(weights):
+    channels = weights.shape[1]
+    by_row = weights.reshape(3, 3 * channels, channels)
+    none = jnp.zeros((1, 3 * channels, channels), weights.dtype)
+    upper = jnp.concatenate([by_row, none], axis=0)
+    lower = jnp.concatenate([none, by_row], axis=0)
+    return jnp.concatenate([upper, lower], axis=-1).reshape(12 * channels, 2 * channels)
+
+
+def transposed(weights):
+    channels = weights.shape[1]
+    taps = weights.reshape(9, channels, channels)[::-1].transpose(0, 2, 1)
+    return taps.reshape(9 * channels, channels)
+
+
+def column_shifts(values):
+    shape = values.shape
+    side, channels = shape[-2], shape[-1]
+    flat = values.reshape(-1, channels)
+    rows = flat.shape[0]
+    column = lax.rem(lax.broadcasted_iota(jnp.int32, flat.shape, 0), side)
+    left = jnp.where(column == 0, 0.0, pltpu.roll(flat, 1, 0))
+    right = jnp.where(column == side - 1, 0.0, pltpu.roll(flat, rows - 1, 0))
+    return [part.astype(jnp.bfloat16).reshape(shape) for part in (left, flat, right)]
+
+
+def put_shifts(padded, values):
+    channels = values.shape[-1]
+    half = values.shape[1]
+    for at, part in enumerate(column_shifts(values)):
+        lanes = slice(at * channels, (at + 1) * channels)
+        padded[:, 0:half, 1, :, lanes] = part[:, :, 0]
+        padded[:, 1 : half + 1, 0, :, lanes] = part[:, :, 1]
+
+
+def conv_rows(padded, weights):
+    half = padded.shape[1] - 1
+    stacked = jnp.concatenate(
+        [padded[:, 0:half, 0], padded[:, 0:half, 1], padded[:, 1:, 0], padded[:, 1:, 1]], axis=-1
+    )
+    lead = stacked.shape[:-1]
+    out = jnp.dot(
+        stacked.reshape(-1, stacked.shape[-1]), weights, preferred_element_type=jnp.float32
+    )
+    channels = weights.shape[1] // 2
+    return (
+        out[:, :channels].reshape(lead + (channels,)),
+        out[:, channels:].reshape(lead + (channels,)),
+    )
+
+
+def clear_edges(padded):
+    shape = padded.shape
+    none = jnp.zeros((shape[0],) + shape[3:], padded.dtype)
+    padded[:, 0, 0] = none
+    padded[:, shape[1] - 1, 1] = none
+
+
+def forward_kernel(
+    maps, in_w, out_w, decay, skip, inputs, states_b, mixed, pooled, padded, states, carried
+):
+    step = pl.program_id(0)
+
+    @pl.when(step == 0)
+    def _():
+        clear_edges(padded)
+        carried[...] = jnp.zeros_like(carried)
+        pooled[...] = jnp.zeros_like(pooled)
+
+    put_shifts(padded, maps[...].astype(jnp.float32))
+    even, odd = conv_rows(padded, in_w[...])
+    inputs[:, :, 0] = even.astype(jnp.bfloat16)
+    inputs[:, :, 1] = odd.astype(jnp.bfloat16)
+    for frame in range(maps.shape[0]):
+        now = decay[frame : frame + 1, :].reshape(1, 1, 1, -1)
+        state = now * carried[...] + inputs[frame].astype(jnp.float32)
+        carried[...] = state
+        states[frame] = state
+        states_b[frame] = state.astype(jnp.bfloat16)
+    put_shifts(padded, states_b[...].astype(jnp.float32))
+    gain = skip[...].reshape(1, 1, 1, -1)
+    total = pooled[...]
+    for parity, out in enumerate(conv_rows(padded, out_w[...])):
+        value = out + gain * inputs[:, :, parity].astype(jnp.float32)
+        mixed[:, :, parity] = value
+        active = value * jax.nn.sigmoid(value)
+        total = total + jnp.sum(active.reshape(-1, 8, active.shape[-1]), axis=0)
+    pooled[...] = total
+
+
+def put_rows(rows, values):
+    frames, half, _, side, channels = values.shape
+    rows[:, 1 : 2 * half + 1] = values.reshape(frames, 2 * half, side, channels)
+
+
+def tap_product(rows, padded):
+    height = rows.shape[1] - 2
+    left = jnp.concatenate([rows[:, k : k + height] for k in range(3)], axis=-1)
+    frames, half = padded.shape[0], padded.shape[1] - 1
+    right = padded[...].reshape(frames, 2 * half + 2, padded.shape[3], padded.shape[4])
+    right = right[:, 1 : 2 * half + 1]
+    return lax.dot_general(
+        left.reshape(-1, left.shape[-1]),
+        right.reshape(-1, right.shape[-1]),
+        (((0,), (0,)), ((), ())),
+        preferred_element_type=jnp.float32,
+    )
+
+
+def backward_kernel(
+    maps, states_b, mixed, dpool, back_w, after, skip, grads, padded, rows, dmix, total, carried
+):
+    step = pl.program_id(0)
+
+    @pl.when(step == 0)
+    def _():
+        clear_edges(padded)
+        rows[:, 0] = jnp.zeros_like(rows[:, 0])
+        rows[:, rows.shape[1] - 1] = jnp.zeros_like(rows[:, 0])
+        carried[...] = jnp.zeros_like(carried)
+        total[...] = jnp.zeros_like(total)
+
+    value = mixed[...]
+    sigma = jax.nn.sigmoid(value)
+    slope = dpool[...].reshape(1, 1, 1, 1, -1)
+    dmix[...] = slope * (sigma * (1.0 + value * (1.0 - sigma)))
+    put_shifts(padded, dmix[...].astype(jnp.bfloat16).astype(jnp.float32))
+    put_rows(rows, states_b[...])
+    total[1] += tap_product(rows, padded)
+    even, odd = conv_rows(padded, back_w[...])
+    gain = skip[...].reshape(1, 1, 1, -1)
+    for frame in reversed(range(maps.shape[0])):
+        now = after[frame : frame + 1, :].reshape(1, 1, -1)
+        for parity, out in enumerate((even, odd)):
+            adjoint = out[frame] + now * carried[:, parity]
+            carried[:, parity] = adjoint
+            dmix[frame, :, parity] = adjoint + gain[0] * dmix[frame, :, parity]
+    put_shifts(padded, dmix[...].astype(jnp.bfloat16).astype(jnp.float32))
+    put_rows(rows, maps[...])
+    total[0] += tap_product(rows, padded)
+
+    @pl.when(step == pl.num_programs(0) - 1)
+    def _():
+        channels = skip.shape[1]
+        for which in range(2):
+            for row in range(3):
+                for col in range(3):
+                    tap = 3 * row + col
+                    grads[which, tap * channels : (tap + 1) * channels, :] = total[
+                        which,
+                        row * channels : (row + 1) * channels,
+                        (2 - col) * channels : (3 - col) * channels,
+                    ]
+
+
+def middle_kernel(pooled, proj_in, gain, proj_out, dpooled):
+    clips = pooled.shape[0] // 2
+    hidden = jnp.dot(
+        pooled[...], proj_in[...], precision=HIGHEST, preferred_element_type=jnp.float32
+    )
+
+    def mean(values):
+        return jnp.sum(values, axis=0, keepdims=True) / clips
+
+    def normed(values):
+        centered = values - mean(values)
+        scale = lax.rsqrt(mean(centered * centered) + EPSILON)
+        return (centered * scale, scale)
+
+    def backed(grad, values, scale):
+        return (grad - mean(grad) - values * mean(grad * values)) * scale
+
+    gains = gain[...]
+    hidden_x, hidden_s, hidden_n = ([], [], [])
+    for view in range(2):
+        values, scale = normed(hidden[view * clips : (view + 1) * clips])
+        hidden_x.append(values)
+        hidden_s.append(scale)
+        hidden_n.append(values * gains)
+    relu_b = jnp.concatenate([jnp.maximum(part, 0.0) for part in hidden_n], axis=0)
+    z_both = jnp.dot(
+        relu_b.astype(jnp.bfloat16), proj_out[...], preferred_element_type=jnp.float32
+    )
+    z_x, z_s, z_n = ([], [], [])
+    for view in range(2):
+        values, scale = normed(z_both[view * clips : (view + 1) * clips])
+        z_x.append(values)
+        z_s.append(scale)
+        z_n.append(values.astype(jnp.bfloat16).astype(jnp.float32))
+    agree = mean(z_n[0] * z_n[1])
+    extra = -2.0 * (1.0 - agree) - 2.0 * LAMBDA_OFF * agree
+    dz = []
+    for view in range(2):
+        mine, other = z_n[view], z_n[1 - view]
+        other_b = other.astype(jnp.bfloat16)
+        gram = lax.dot_general(
+            other_b, other_b, (((1,), (1,)), ((), ())), preferred_element_type=jnp.float32
+        )
+        spread = jnp.dot(
+            gram * (2.0 * LAMBDA_OFF / clips),
+            mine,
+            precision=HIGHEST,
+            preferred_element_type=jnp.float32,
+        )
+        dzn = (spread + other * extra) / clips
+        dz.append(backed(dzn, z_x[view], z_s[view]))
+    drelu = lax.dot_general(
+        jnp.concatenate(dz, axis=0).astype(jnp.bfloat16),
+        proj_out[...],
+        (((1,), (1,)), ((), ())),
+        preferred_element_type=jnp.float32,
+    )
+    dhidden = []
+    for view in range(2):
+        part = drelu[view * clips : (view + 1) * clips]
+        dxh = jnp.where(hidden_n[view] > 0, part, 0.0) * gains
+        dhidden.append(backed(dxh, hidden_x[view], hidden_s[view]))
+    dpooled[...] = lax.dot_general(
+        jnp.concatenate(dhidden, axis=0),
+        proj_in[...],
+        (((1,), (1,)), ((), ())),
+        precision=HIGHEST,
+        preferred_element_type=jnp.float32,
+    )
+
+
+def forward(maps, in_w, out_w, decay, skip):
+    frames, half, _, side, channels = maps.shape
+    steps = frames // BLOCK
+    shape = (BLOCK, half, 2, side, channels)
+    frame_spec = pl.BlockSpec(shape, lambda i: (i, 0, 0, 0, 0))
+    whole = pl.BlockSpec(memory_space=pltpu.VMEM)
+    return pl.pallas_call(
+        forward_kernel,
+        grid=(steps,),
+        in_specs=[
+            frame_spec,
+            whole,
+            whole,
+            pl.BlockSpec((BLOCK, channels), lambda i: (i, 0)),
+            whole,
+        ],
+        out_specs=[frame_spec, frame_spec, frame_spec, whole],
+        out_shape=[
+            jax.ShapeDtypeStruct(maps.shape, jnp.bfloat16),
+            jax.ShapeDtypeStruct(maps.shape, jnp.bfloat16),
+            jax.ShapeDtypeStruct(maps.shape, jnp.float32),
+            jax.ShapeDtypeStruct((8, channels), jnp.float32),
+        ],
+        scratch_shapes=[
+            pltpu.VMEM((BLOCK, half + 1, 2, side, 3 * channels), jnp.bfloat16),
+            pltpu.VMEM(shape, jnp.float32),
+            pltpu.VMEM(shape[1:], jnp.float32),
+        ],
+        compiler_params=pltpu.CompilerParams(vmem_limit_bytes=VMEM_BYTES),
+    )(maps, pair_weights(in_w), pair_weights(out_w), decay, skip)
+
+
+def backward(maps, states_b, mixed, dpool, out_w, decay, skip):
+    frames, half, _, side, channels = maps.shape
+    steps = frames // BLOCK
+    shape = (BLOCK, half, 2, side, channels)
+    frame_spec = pl.BlockSpec(shape, lambda i: (steps - 1 - i, 0, 0, 0, 0))
+    whole = pl.BlockSpec(memory_space=pltpu.VMEM)
+    after = jnp.concatenate([decay[1:], jnp.zeros((1, channels), jnp.float32)], axis=0)
+    return pl.pallas_call(
+        backward_kernel,
+        grid=(steps,),
+        in_specs=[
+            frame_spec,
+            frame_spec,
+            frame_spec,
+            whole,
+            whole,
+            pl.BlockSpec((BLOCK, channels), lambda i: (steps - 1 - i, 0)),
+            whole,
+        ],
+        out_specs=whole,
+        out_shape=jax.ShapeDtypeStruct((2, 9 * channels, channels), jnp.float32),
+        scratch_shapes=[
+            pltpu.VMEM((BLOCK, half + 1, 2, side, 3 * channels), jnp.bfloat16),
+            pltpu.VMEM((BLOCK, 2 * half + 2, side, channels), jnp.bfloat16),
+            pltpu.VMEM(shape, jnp.float32),
+            pltpu.VMEM((2, 3 * channels, 3 * channels), jnp.float32),
+            pltpu.VMEM(shape[1:], jnp.float32),
+        ],
+        compiler_params=pltpu.CompilerParams(vmem_limit_bytes=VMEM_BYTES),
+    )(maps, states_b, mixed, dpool, pair_weights(transposed(out_w)), after, skip)
+
+
+def middle(pooled, proj_in, proj_gain, proj_out):
+    whole = pl.BlockSpec(memory_space=pltpu.VMEM)
+    return pl.pallas_call(
+        middle_kernel,
+        in_specs=[whole] * 4,
+        out_specs=whole,
+        out_shape=jax.ShapeDtypeStruct(pooled.shape, jnp.float32),
+        compiler_params=pltpu.CompilerParams(vmem_limit_bytes=VMEM_BYTES),
+    )(pooled, proj_in, proj_gain[None], proj_out)
+
+
+def clip_per_device(
+    rgb_maps, flow_maps, in_weights, out_weights, decay, skip, proj_in, proj_gain, proj_out
+):
+    clips, frames_here, side, _, channels = rgb_maps.shape
+    peers, here = (lax.axis_size("tm"), lax.axis_index("tm"))
+    rings, ring = (lax.axis_size("batch"), lax.axis_index("batch"))
+    frames = frames_here * peers
+    view, clip = (here // clips, here % clips)
+    maps, decay_v = exchange(rgb_maps, flow_maps, decay)
+    maps = maps.reshape(frames, side // 2, 2, side, channels)
+
+    def own(values):
+        return lax.dynamic_index_in_dim(values, view, 0, keepdims=False)
+
+    in_w, out_w, skip_v = (own(in_weights), own(out_weights), own(skip))
+    cells = frames * side * side
+    _, states_b, mixed, pooled = forward(maps, in_w, out_w, decay_v, skip_v[None])
+    gathered = jnp.sum(gather(pooled), axis=2) / cells
+    gathered = gathered.reshape(rings, 2, clips, channels).transpose(1, 0, 2, 3)
+    dpooled = middle(gathered.reshape(-1, channels), proj_in, proj_gain, proj_out)
+    row = (view * rings + ring) * clips + clip
+    dpool = lax.dynamic_slice_in_dim(dpooled, row, 1, 0) / cells
+    grads = backward(maps, states_b, mixed, dpool, out_w, decay_v, skip_v[None])
+    whole = reduce_grads(grads.reshape(-1, channels)).astype(jnp.float32)
+    whole = whole.reshape(2, 2, 9 * channels, channels)
+    return (whole[:, 0], whole[:, 1])
+
+
+def per_device(rgb_maps, *others):
+    clips, frames_here, side = rgb_maps.shape[:3]
+    fits = lax.axis_size("tm") == 2 * clips and side % 2 == 0
+    fits = fits and clips == 4 and (9 * rgb_maps.shape[-1]) % (32 * lax.axis_size("batch")) == 0
+    fits = fits and (frames_here * lax.axis_size("tm")) % BLOCK == 0
+    chosen = clip_per_device if fits else scanned_per_device
+    return chosen(rgb_maps, *others)
+
+
 def solution(mesh):
     return jax.shard_map(
         per_device,

time: 685 us -> 197 us (0.29); the launches traced: 676 us -> 196 us
  blocking collectives: 190 us -> 0 us
  Pallas kernels: 0 us -> 185 us
  waiting for transfers between devices: 167 us -> 0 us
  matrix products: 117 us -> 0 us
  local copies, waits for them, and re-layouts: 100 us -> 4.68 us
  other arithmetic: 85 us -> 6.44 us
  between operations: 15.3 us -> 0.72 us
    pallas_call x0 -> x6, Pallas kernels: none -> 185 us  [the longest x1 50.3 us: exchange(): pl.pallas_call(exchange_kernel, in_specs=[pl.BlockSpec(memory_space=pl.AN...]
    psum x8 -> x0, blocking collectives: 137 us -> none  [the longest x1 23.6 us: per_device(): lax.psum(jnp.dot(block_wide, grad_block, precision=HIGHEST) / clip_total,...]
    dot_general x21 -> x0, matrix products: 117 us -> none  [the longest x6 46.1 us: convolve(): result = jnp.dot(flat, weights, preferred_element_type=jnp.float32)]
    all_gather x6 -> x0, waiting for transfers between devices: 91.1 us -> none  [the longest x4 40.1 us: prefix(): everything = jax.tree.map(lambda part: lax.all_gather(part, axis), x)]
    unnamed x149 -> x4, local copies, waits for them, and re-layouts: 73 us -> 0.01 us
    all_gather x5 -> x0, blocking collectives: 53 us -> none  [the longest x2 19 us: prefix(): everything = jax.tree.map(lambda part: lax.all_gather(part, axis), x)]
    psum x1 -> x0, waiting for transfers between devices: 38.4 us -> none  [per_device(): share_sums = lax.psum((shares[0], shares[1]), 'batch')]
    reduce_scatter x2 -> x0, waiting for transfers between devices: 37 us -> none  [the longest x1 37 us: per_device(): lax.psum_scatter(in_stack, 'tm', scatter_dimension=1, tiled=True)]
  transfers between devices with their start and end apart: 9 -> 0, of which waited for: 6 -> 0; matrix products, arithmetic and copies ran while one was open for 20% -> 0% of each run, Pallas kernels for 0% -> 0%
where the time goes in v1:
time: 197 us; the launch traced here: 196 us
  Pallas kernels  185 us (94%)
  other arithmetic  6.44 us (3%)
  local copies, waits for them, and re-layouts  4.68 us (2%)
    pallas_call x1, Pallas kernels, exchange(): pl.pallas_call(exchange_kernel, in_specs=[pl.BlockSpec(memory_space=pl.AN...  50.3 us
    pallas_call x1, Pallas kernels, backward(): pl.pallas_call(backward_kernel, grid=(steps,), in_specs=[frame_spec, fram...  44.5 us
    pallas_call x1, Pallas kernels, reduce_grads(): pl.pallas_call(reduce_kernel, in_specs=[pl.BlockSpec(memory_space=pltpu.V...  35.6 us
    pallas_call x1, Pallas kernels, forward(): pl.pallas_call(forward_kernel, grid=(steps,), in_specs=[frame_spec, whole...  30.5 us
    pallas_call x1, Pallas kernels, gather(): pl.pallas_call(gather_kernel, in_specs=[pl.BlockSpec(memory_space=pltpu.V...  13 us
    pallas_call x1, Pallas kernels, middle(): pl.pallas_call(middle_kernel, in_specs=[whole] * 4, out_specs=whole, out_...  10.8 us

profile of v1, /device:TPU:0, one launch (start us, length us, event | category | flops | bytes accessed | tf_op | source)
XLA Modules:
  0.0 196.5 jit_solution(12725949373532162403)
XLA Ops:
  0.6 0.0 copy-start
  0.7 1.1 constant_dynamic-slice_fusion.2
  1.8 0.9 fusion.6
  2.7 0.9 fusion.7
  3.7 0.0 copy-done
  3.7 0.5 constant_dynamic-slice_fusion.1.skip
  4.2 50.3 %shard_map.104 = (bf16[64,16,16,128]{3,2,1,0:T(8,128)(2,1)}, f32[64,128]{1,0:T(8,128)}) custom-call(bf16[4,8,16,16,128]{4,3,2,1,0:T(8,128)(2,1)} %rgb.1, bf16[4,8,16,16,128]{4,3,2,1,0:T(8,128)(2,1)} %flow.1, f32[2,8,128]{2,1,0:T(8,128)} %decay.1), custom_call_target="tpu_custom_call" | custom-call | tf_op jit(solution)/shard_map/pallas_call | solution.py:371
  54.5 30.5 %shard_map.105 = (bf16[64,8,2,16,128]{4,3,2,1,0:T(8,128)(2,1)}, bf16[64,8,2,16,128]{4,3,2,1,0:T(8,128)(2,1)}, f32[64,8,2,16,128]{4,3,2,1,0:T(8,128)}, f32[8,128]{1,0:T(8,128)}) custom-call(bf16[64,8,2,16,128]{4,3,2,1,0:T(8,128)(2,1)} %bitcast.27, bf16[1536,256]{1,0:T(8,128)(2,1)} %bitcast.31, bf16[1536,256]{1,0:T(8,128)(2,1)} %bitcast.32, ...), custom_call_target="tpu_custom_call" | custom-call | tf_op jit(solution)/shard_map/pallas_call | solution.py:748
  85.0 13.0 %shard_map.106 = f32[4,8,8,128]{3,2,1,0:T(8,128)} custom-call(f32[8,128]{1,0:T(8,128)} %get-tuple-element.11.pooled), custom_call_target="tpu_custom_call" | custom-call | tf_op jit(solution)/shard_map/pallas_call | solution.py:416
  98.0 0.9 reduce_sum.9
  99.0 0.6 copy.16
  99.6 10.8 %shard_map.107 = f32[32,128]{1,0:T(8,128)} custom-call(f32[32,128]{1,0:T(8,128)} %bitcast.37, f32[128,2048]{1,0:T(8,128)} %proj_in.1, f32[1,2048]{1,0:T(1,128)} %bitcast.39, bf16[2048,2048]{1,0:T(8,128)(2,1)} %proj_out.1), custom_call_target="tpu_custom_call" | custom-call | tf_op jit(solution)/shard_map/pallas_call | solution.py:808
  110.3 0.0 copy-start.1
  110.3 1.2 fusion.9.dpool
  111.6 0.2 copy.17
  111.8 1.0 fusion.8
  112.7 0.0 copy-done.1
  112.8 0.6 concatenate.39.after
  113.4 44.5 %shard_map.108 = f32[2,1152,128]{2,1,0:T(8,128)} custom-call(bf16[64,8,2,16,128]{4,3,2,1,0:T(8,128)(2,1)} %bitcast.28, bf16[64,8,2,16,128]{4,3,2,1,0:T(8,128)(2,1)} %get-tuple-element.9.states_b, f32[64,8,2,16,128]{4,3,2,1,0:T(8,128)} %get-tuple-element.10.mixed, f32[1,128]{1,0:T(1,128)} %fusion.9.dpool, bf16[1536,256]{1,0:T(8,128)(2,1)} %bitcast.30, ...), custom_call_target="tpu_custom_call" | custom-call | tf_op jit(solution)/shard_map/pallas_call | solution.py:781
  157.9 35.6 %shard_map.109 = bf16[2,2,2,4,144,128]{5,4,3,2,1,0:T(8,128)(2,1)} custom-call(f32[2,2,4,144,128]{4,3,2,1,0:T(8,128)} %bitcast.29), custom_call_target="tpu_custom_call" | custom-call | tf_op jit(solution)/shard_map/pallas_call | solution.py:496
  193.5 1.4 bitcast_convert_fusion
  194.9 1.6 slice_bitcast_fusion
  (3 shorter events, 0.0 us)
Async XLA Ops:
  0.6 3.0 %copy-start = (f32[2,128]{1,0:T(2,128)S(1)}, f32[2,128]{1,0:T(2,128)}, u32[]{:S(2)}) copy-start(f32[2,128]{1,0:T(2,128)} %param.14) | copy-start | bytes 3076
  110.3 2.4 %copy-start.1 = (f32[64,128]{1,0:T(8,128)S(1)}, f32[64,128]{1,0:T(8,128)}, u32[]{:S(2)}) copy-start(f32[64,128]{1,0:T(8,128)} %get-tuple-element.8.decay) | copy-start | bytes 98308

commit v2 on v1

--- a/solution.py
+++ b/solution.py
@@ -513,55 +513,48 @@
     )(grads.reshape((2, 2) + part))
 
 
-def pair_weights(weights):
-    channels = weights.shape[1]
-    by_row = weights.reshape(3, 3 * channels, channels)
-    none = jnp.zeros((1, 3 * channels, channels), weights.dtype)
-    upper = jnp.concatenate([by_row, none], axis=0)
-    lower = jnp.concatenate([none, by_row], axis=0)
-    return jnp.concatenate([upper, lower], axis=-1).reshape(12 * channels, 2 * channels)
-
-
-def transposed(weights):
-    channels = weights.shape[1]
-    taps = weights.reshape(9, channels, channels)[::-1].transpose(0, 2, 1)
-    return taps.reshape(9 * channels, channels)
-
-
-def column_shifts(values):
-    shape = values.shape
-    side, channels = shape[-2], shape[-1]
-    flat = values.reshape(-1, channels)
-    rows = flat.shape[0]
-    column = lax.rem(lax.broadcasted_iota(jnp.int32, flat.shape, 0), side)
-    left = jnp.where(column == 0, 0.0, pltpu.roll(flat, 1, 0))
-    right = jnp.where(column == side - 1, 0.0, pltpu.roll(flat, rows - 1, 0))
-    return [part.astype(jnp.bfloat16).reshape(shape) for part in (left, flat, right)]
-
-
-def put_shifts(padded, values):
-    channels = values.shape[-1]
-    half = values.shape[1]
-    for at, part in enumerate(column_shifts(values)):
+def put_pairs(pairs, tap):
+    channels = pairs.shape[1] // 2
+    pairs[...] = jnp.zeros_like(pairs)
+    for k in range(9):
+        weights = tap(k)
+        pairs[k * channels : (k + 1) * channels, :channels] = weights
+        pairs[(k + 3) * channels : (k + 4) * channels, channels:] = weights
+
+
+def tap_reader(weights, view):
+    channels = weights.shape[2]
+    return lambda k: weights[view, k * channels : (k + 1) * channels, :]
+
+
+def put_shifts(padded, frame, values):
+    half, _, side, channels = values.shape
+    rounded = values.astype(jnp.bfloat16)
+    wide = rounded.astype(jnp.float32).reshape(2 * half, side, channels)
+    column = lax.broadcasted_iota(jnp.int32, (1, side, channels), 1)
+    left = jnp.where(column == 0, 0.0, pltpu.roll(wide, 1, 1)).astype(jnp.bfloat16)
+    right = jnp.where(column == side - 1, 0.0, pltpu.roll(wide, side - 1, 1)).astype(jnp.bfloat16)
+    for at, part in enumerate((left, rounded, right)):
+        part = part.reshape(values.shape)
         lanes = slice(at * channels, (at + 1) * channels)
-        padded[:, 0:half, 1, :, lanes] = part[:, :, 0]
-        padded[:, 1 : half + 1, 0, :, lanes] = part[:, :, 1]
-
-
-def conv_rows(padded, weights):
+        padded[frame, 0:half, 1, :, lanes] = part[:, 0]
+        padded[frame, 1 : half + 1, 0, :, lanes] = part[:, 1]
+    return rounded
+
+
+def four_rows(padded):
     half = padded.shape[1] - 1
     stacked = jnp.concatenate(
         [padded[:, 0:half, 0], padded[:, 0:half, 1], padded[:, 1:, 0], padded[:, 1:, 1]], axis=-1
     )
-    lead = stacked.shape[:-1]
-    out = jnp.dot(
-        stacked.reshape(-1, stacked.shape[-1]), weights, preferred_element_type=jnp.float32
-    )
-    channels = weights.shape[1] // 2
-    return (
-        out[:, :channels].reshape(lead + (channels,)),
-        out[:, channels:].reshape(lead + (channels,)),
-    )
+    return stacked.reshape(-1, stacked.shape[-1])
+
+
+def conv_rows(padded, pairs):
+    out = jnp.dot(four_rows(padded), pairs[...], preferred_element_type=jnp.float32)
+    channels = pairs.shape[1] // 2
+    shape = (padded.shape[0], padded.shape[1] - 1, padded.shape[3], channels)
+    return (out[:, :channels].reshape(shape), out[:, channels:].reshape(shape))
 
 
 def clear_edges(padded):
@@ -571,111 +564,142 @@
     padded[:, shape[1] - 1, 1] = none
 
 
+def sigmoid(values):
+    return 0.5 + 0.5 * jnp.tanh(0.5 * values)
+
+
 def forward_kernel(
-    maps, in_w, out_w, decay, skip, inputs, states_b, mixed, pooled, padded, states, carried
+    maps,
+    in_w,
+    out_w,
+    decay,
+    skip,
+    states_b,
+    slope,
+    pooled,
+    in_pairs,
+    out_pairs,
+    padded,
+    inputs,
+    carried,
 ):
     step = pl.program_id(0)
+    view = lax.axis_index("tm") // (lax.axis_size("tm") // 2)
 
     @pl.when(step == 0)
     def _():
+        put_pairs(in_pairs, tap_reader(in_w, view))
+        put_pairs(out_pairs, tap_reader(out_w, view))
         clear_edges(padded)
         carried[...] = jnp.zeros_like(carried)
         pooled[...] = jnp.zeros_like(pooled)
 
-    put_shifts(padded, maps[...].astype(jnp.float32))
-    even, odd = conv_rows(padded, in_w[...])
+    for frame in range(maps.shape[0]):
+        put_shifts(padded, frame, maps[frame])
+    even, odd = conv_rows(padded, in_pairs)
     inputs[:, :, 0] = even.astype(jnp.bfloat16)
     inputs[:, :, 1] = odd.astype(jnp.bfloat16)
     for frame in range(maps.shape[0]):
         now = decay[frame : frame + 1, :].reshape(1, 1, 1, -1)
         state = now * carried[...] + inputs[frame].astype(jnp.float32)
         carried[...] = state
-        states[frame] = state
-        states_b[frame] = state.astype(jnp.bfloat16)
-    put_shifts(padded, states_b[...].astype(jnp.float32))
-    gain = skip[...].reshape(1, 1, 1, -1)
+        states_b[frame] = put_shifts(padded, frame, state)
+    gain = skip[pl.ds(view, 1), :].reshape(1, 1, 1, -1)
     total = pooled[...]
-    for parity, out in enumerate(conv_rows(padded, out_w[...])):
+    for parity, out in enumerate(conv_rows(padded, out_pairs)):
         value = out + gain * inputs[:, :, parity].astype(jnp.float32)
-        mixed[:, :, parity] = value
-        active = value * jax.nn.sigmoid(value)
+        sigma = sigmoid(value)
+        active = value * sigma
+        slope[:, :, parity] = sigma + active * (1.0 - sigma)
         total = total + jnp.sum(active.reshape(-1, 8, active.shape[-1]), axis=0)
     pooled[...] = total
 
 
-def put_rows(rows, values):
-    frames, half, _, side, channels = values.shape
-    rows[:, 1 : 2 * half + 1] = values.reshape(frames, 2 * half, side, channels)
-
-
-def tap_product(rows, padded):
-    height = rows.shape[1] - 2
-    left = jnp.concatenate([rows[:, k : k + height] for k in range(3)], axis=-1)
-    frames, half = padded.shape[0], padded.shape[1] - 1
-    right = padded[...].reshape(frames, 2 * half + 2, padded.shape[3], padded.shape[4])
-    right = right[:, 1 : 2 * half + 1]
-    return lax.dot_general(
-        left.reshape(-1, left.shape[-1]),
-        right.reshape(-1, right.shape[-1]),
-        (((0,), (0,)), ((), ())),
-        preferred_element_type=jnp.float32,
-    )
-
-
 def backward_kernel(
-    maps, states_b, mixed, dpool, back_w, after, skip, grads, padded, rows, dmix, total, carried
+    maps,
+    states_b,
+    slope,
+    dpooled,
+    out_w,
+    decay,
+    skip,
+    grads,
+    pairs,
+    padded,
+    dmix,
+    total,
+    carried,
 ):
-    step = pl.program_id(0)
+    step, steps = (pl.program_id(0), pl.num_programs(0))
+    me, peers = (lax.axis_index("tm"), lax.axis_size("tm"))
+    view = me // (peers // 2)
+    block, half, _, side, channels = maps.shape
+    frames = decay.shape[0]
 
     @pl.when(step == 0)
     def _():
+        read = tap_reader(out_w, view)
+        put_pairs(pairs, lambda k: read(8 - k).astype(jnp.float32).T.astype(jnp.bfloat16))
         clear_edges(padded)
-        rows[:, 0] = jnp.zeros_like(rows[:, 0])
-        rows[:, rows.shape[1] - 1] = jnp.zeros_like(rows[:, 0])
         carried[...] = jnp.zeros_like(carried)
         total[...] = jnp.zeros_like(total)
 
-    value = mixed[...]
-    sigma = jax.nn.sigmoid(value)
-    slope = dpool[...].reshape(1, 1, 1, 1, -1)
-    dmix[...] = slope * (sigma * (1.0 + value * (1.0 - sigma)))
-    put_shifts(padded, dmix[...].astype(jnp.bfloat16).astype(jnp.float32))
-    put_rows(rows, states_b[...])
-    total[1] += tap_product(rows, padded)
-    even, odd = conv_rows(padded, back_w[...])
-    gain = skip[...].reshape(1, 1, 1, -1)
-    for frame in reversed(range(maps.shape[0])):
-        now = after[frame : frame + 1, :].reshape(1, 1, -1)
+    def tap_product(values):
+        both = jnp.concatenate([values[:, :, 0], values[:, :, 1]], axis=-1)
+        return lax.dot_general(
+            both.reshape(-1, 2 * channels),
+            four_rows(padded),
+            (((0,), (0,)), ((), ())),
+            preferred_element_type=jnp.float32,
+        )
+
+    row = lax.axis_index("batch") * peers + me
+    share = (dpooled[pl.ds(row, 1), :] / (frames * 2 * half * side)).reshape(1, 1, 1, -1)
+    gain = skip[pl.ds(view, 1), :].reshape(1, 1, 1, -1)
+    for frame in range(block):
+        part = share * slope[frame]
+        dmix[frame] = gain * part
+        put_shifts(padded, frame, part)
+    total[1] += tap_product(states_b[...])
+    even, odd = conv_rows(padded, pairs)
+    first = (steps - 1 - step) * block
+    for frame in reversed(range(block)):
+        now = decay[pl.ds(jnp.minimum(first + frame + 1, frames - 1), 1), :].reshape(1, 1, -1)
         for parity, out in enumerate((even, odd)):
             adjoint = out[frame] + now * carried[:, parity]
             carried[:, parity] = adjoint
-            dmix[frame, :, parity] = adjoint + gain[0] * dmix[frame, :, parity]
-    put_shifts(padded, dmix[...].astype(jnp.bfloat16).astype(jnp.float32))
-    put_rows(rows, maps[...])
-    total[0] += tap_product(rows, padded)
-
-    @pl.when(step == pl.num_programs(0) - 1)
+            dmix[frame, :, parity] += adjoint
+        put_shifts(padded, frame, dmix[frame])
+    total[0] += tap_product(maps[...])
+
+    @pl.when(step == steps - 1)
     def _():
-        channels = skip.shape[1]
         for which in range(2):
-            for row in range(3):
-                for col in range(3):
-                    tap = 3 * row + col
-                    grads[which, tap * channels : (tap + 1) * channels, :] = total[
-                        which,
-                        row * channels : (row + 1) * channels,
-                        (2 - col) * channels : (3 - col) * channels,
-                    ]
-
-
-def middle_kernel(pooled, proj_in, gain, proj_out, dpooled):
-    clips = pooled.shape[0] // 2
-    hidden = jnp.dot(
-        pooled[...], proj_in[...], precision=HIGHEST, preferred_element_type=jnp.float32
-    )
+            for row_off in range(3):
+                for col_off in range(3):
+                    tap = 3 * row_off + col_off
+                    summed = 0.0
+                    for parity in range(2):
+                        at = (3 * (2 + parity - row_off) + 2 - col_off) * channels
+                        summed += total[
+                            which, parity * channels : (parity + 1) * channels, at : at + channels
+                        ]
+                    grads[which, tap * channels : (tap + 1) * channels, :] = summed
+
+
+def middle_kernel(cells, everyone, proj_in, gain, proj_out, dpooled):
+    rings, peers, _, channels = everyone.shape
+    rows, per_view = (rings * peers, peers // 2)
+    clips = rings * per_view
+    width = proj_out.shape[1]
+    pooled = (jnp.sum(everyone[...], axis=2) / cells).reshape(rows, channels)
+    place = lax.broadcasted_iota(jnp.int32, (rows, width), 0)
+    rgb = lax.rem(place, peers) < per_view
 
     def mean(values):
-        return jnp.sum(values, axis=0, keepdims=True) / clips
+        of_rgb = jnp.sum(jnp.where(rgb, values, 0.0), axis=0, keepdims=True) / clips
+        of_flow = jnp.sum(jnp.where(rgb, 0.0, values), axis=0, keepdims=True) / clips
+        return jnp.where(rgb, of_rgb, of_flow)
 
     def normed(values):
         centered = values - mean(values)
@@ -685,53 +709,33 @@
     def backed(grad, values, scale):
         return (grad - mean(grad) - values * mean(grad * values)) * scale
 
-    gains = gain[...]
-    hidden_x, hidden_s, hidden_n = ([], [], [])
-    for view in range(2):
-        values, scale = normed(hidden[view * clips : (view + 1) * clips])
-        hidden_x.append(values)
-        hidden_s.append(scale)
-        hidden_n.append(values * gains)
-    relu_b = jnp.concatenate([jnp.maximum(part, 0.0) for part in hidden_n], axis=0)
-    z_both = jnp.dot(
-        relu_b.astype(jnp.bfloat16), proj_out[...], preferred_element_type=jnp.float32
-    )
-    z_x, z_s, z_n = ([], [], [])
-    for view in range(2):
-        values, scale = normed(z_both[view * clips : (view + 1) * clips])
-        z_x.append(values)
-        z_s.append(scale)
-        z_n.append(values.astype(jnp.bfloat16).astype(jnp.float32))
-    agree = mean(z_n[0] * z_n[1])
+    hidden = jnp.dot(pooled, proj_in[...], precision=HIGHEST, preferred_element_type=jnp.float32)
+    hidden_x, hidden_s = normed(hidden)
+    hidden_n = hidden_x * gain[...]
+    relu_b = jnp.maximum(hidden_n, 0.0).astype(jnp.bfloat16)
+    z_x, z_s = normed(jnp.dot(relu_b, proj_out[...], preferred_element_type=jnp.float32))
+    z_n = z_x.astype(jnp.bfloat16).astype(jnp.float32)
+    other = pltpu.roll(z_n.reshape(rings, peers, width), per_view, 1).reshape(rows, width)
+    agree = jnp.sum(jnp.where(rgb, z_n * other, 0.0), axis=0, keepdims=True) / clips
     extra = -2.0 * (1.0 - agree) - 2.0 * LAMBDA_OFF * agree
-    dz = []
-    for view in range(2):
-        mine, other = z_n[view], z_n[1 - view]
-        other_b = other.astype(jnp.bfloat16)
-        gram = lax.dot_general(
-            other_b, other_b, (((1,), (1,)), ((), ())), preferred_element_type=jnp.float32
-        )
-        spread = jnp.dot(
-            gram * (2.0 * LAMBDA_OFF / clips),
-            mine,
-            precision=HIGHEST,
-            preferred_element_type=jnp.float32,
-        )
-        dzn = (spread + other * extra) / clips
-        dz.append(backed(dzn, z_x[view], z_s[view]))
+    other_b = other.astype(jnp.bfloat16)
+    gram = lax.dot_general(
+        other_b, other_b, (((1,), (1,)), ((), ())), preferred_element_type=jnp.float32
+    )
+    down = lax.rem(lax.broadcasted_iota(jnp.int32, (rows, rows), 0), peers) < per_view
+    along = lax.rem(lax.broadcasted_iota(jnp.int32, (rows, rows), 1), peers) < per_view
+    gram = jnp.where(down == along, gram, 0.0) * (2.0 * LAMBDA_OFF / clips)
+    spread = jnp.dot(gram, z_n, precision=HIGHEST, preferred_element_type=jnp.float32)
+    dz = backed((spread + other * extra) / clips, z_x, z_s)
     drelu = lax.dot_general(
-        jnp.concatenate(dz, axis=0).astype(jnp.bfloat16),
+        dz.astype(jnp.bfloat16),
         proj_out[...],
         (((1,), (1,)), ((), ())),
         preferred_element_type=jnp.float32,
     )
-    dhidden = []
-    for view in range(2):
-        part = drelu[view * clips : (view + 1) * clips]
-        dxh = jnp.where(hidden_n[view] > 0, part, 0.0) * gains
-        dhidden.append(backed(dxh, hidden_x[view], hidden_s[view]))
+    dhidden = backed(jnp.where(hidden_n > 0, drelu, 0.0) * gain[...], hidden_x, hidden_s)
     dpooled[...] = lax.dot_general(
-        jnp.concatenate(dhidden, axis=0),
+        dhidden,
         proj_in[...],
         (((1,), (1,)), ((), ())),
         precision=HIGHEST,
@@ -741,13 +745,13 @@
 
 def forward(maps, in_w, out_w, decay, skip):
     frames, half, _, side, channels = maps.shape
-    steps = frames // BLOCK
     shape = (BLOCK, half, 2, side, channels)
     frame_spec = pl.BlockSpec(shape, lambda i: (i, 0, 0, 0, 0))
     whole = pl.BlockSpec(memory_space=pltpu.VMEM)
+    pairs = pltpu.VMEM((12 * channels, 2 * channels), jnp.bfloat16)
     return pl.pallas_call(
         forward_kernel,
-        grid=(steps,),
+        grid=(frames // BLOCK,),
         in_specs=[
             frame_spec,
             whole,
@@ -755,88 +759,68 @@
             pl.BlockSpec((BLOCK, channels), lambda i: (i, 0)),
             whole,
         ],
-        out_specs=[frame_spec, frame_spec, frame_spec, whole],
+        out_specs=[frame_spec, frame_spec, whole],
         out_shape=[
-            jax.ShapeDtypeStruct(maps.shape, jnp.bfloat16),
             jax.ShapeDtypeStruct(maps.shape, jnp.bfloat16),
             jax.ShapeDtypeStruct(maps.shape, jnp.float32),
             jax.ShapeDtypeStruct((8, channels), jnp.float32),
         ],
         scratch_shapes=[
+            pairs,
+            pairs,
             pltpu.VMEM((BLOCK, half + 1, 2, side, 3 * channels), jnp.bfloat16),
-            pltpu.VMEM(shape, jnp.float32),
+            pltpu.VMEM(shape, jnp.bfloat16),
             pltpu.VMEM(shape[1:], jnp.float32),
         ],
         compiler_params=pltpu.CompilerParams(vmem_limit_bytes=VMEM_BYTES),
-    )(maps, pair_weights(in_w), pair_weights(out_w), decay, skip)
-
-
-def backward(maps, states_b, mixed, dpool, out_w, decay, skip):
+    )(maps, in_w, out_w, decay, skip)
+
+
+def backward(maps, states_b, slope, dpooled, out_w, decay, skip):
     frames, half, _, side, channels = maps.shape
     steps = frames // BLOCK
     shape = (BLOCK, half, 2, side, channels)
     frame_spec = pl.BlockSpec(shape, lambda i: (steps - 1 - i, 0, 0, 0, 0))
     whole = pl.BlockSpec(memory_space=pltpu.VMEM)
-    after = jnp.concatenate([decay[1:], jnp.zeros((1, channels), jnp.float32)], axis=0)
     return pl.pallas_call(
         backward_kernel,
         grid=(steps,),
-        in_specs=[
-            frame_spec,
-            frame_spec,
-            frame_spec,
-            whole,
-            whole,
-            pl.BlockSpec((BLOCK, channels), lambda i: (steps - 1 - i, 0)),
-            whole,
-        ],
+        in_specs=[frame_spec, frame_spec, frame_spec, whole, whole, whole, whole],
         out_specs=whole,
         out_shape=jax.ShapeDtypeStruct((2, 9 * channels, channels), jnp.float32),
         scratch_shapes=[
+            pltpu.VMEM((12 * channels, 2 * channels), jnp.bfloat16),
             pltpu.VMEM((BLOCK, half + 1, 2, side, 3 * channels), jnp.bfloat16),
-            pltpu.VMEM((BLOCK, 2 * half + 2, side, channels), jnp.bfloat16),
             pltpu.VMEM(shape, jnp.float32),
-            pltpu.VMEM((2, 3 * channels, 3 * channels), jnp.float32),
+            pltpu.VMEM((2, 2 * channels, 12 * channels), jnp.float32),
             pltpu.VMEM(shape[1:], jnp.float32),
         ],
         compiler_params=pltpu.CompilerParams(vmem_limit_bytes=VMEM_BYTES),
-    )(maps, states_b, mixed, dpool, pair_weights(transposed(out_w)), after, skip)
-
-
-def middle(pooled, proj_in, proj_gain, proj_out):
+    )(maps, states_b, slope, dpooled, out_w, decay, skip)
+
+
+def middle(everyone, cells, proj_in, proj_gain, proj_out):
+    rings, peers, _, channels = everyone.shape
     whole = pl.BlockSpec(memory_space=pltpu.VMEM)
     return pl.pallas_call(
-        middle_kernel,
+        functools.partial(middle_kernel, cells),
         in_specs=[whole] * 4,
         out_specs=whole,
-        out_shape=jax.ShapeDtypeStruct(pooled.shape, jnp.float32),
+        out_shape=jax.ShapeDtypeStruct((rings * peers, channels), jnp.float32),
         compiler_params=pltpu.CompilerParams(vmem_limit_bytes=VMEM_BYTES),
-    )(pooled, proj_in, proj_gain[None], proj_out)
+    )(everyone, proj_in, proj_gain[None], proj_out)
 
 
 def clip_per_device(
     rgb_maps, flow_maps, in_weights, out_weights, decay, skip, proj_in, proj_gain, proj_out
 ):
-    clips, frames_here, side, _, channels = rgb_maps.shape
-    peers, here = (lax.axis_size("tm"), lax.axis_index("tm"))
-    rings, ring = (lax.axis_size("batch"), lax.axis_index("batch"))
-    frames = frames_here * peers
-    view, clip = (here // clips, here % clips)
-    maps, decay_v = exchange(rgb_maps, flow_maps, decay)
+    side, channels = rgb_maps.shape[-2:]
+    maps, decays = exchange(rgb_maps, flow_maps, decay)
+    frames = maps.shape[0]
     maps = maps.reshape(frames, side // 2, 2, side, channels)
-
-    def own(values):
-        return lax.dynamic_index_in_dim(values, view, 0, keepdims=False)
-
-    in_w, out_w, skip_v = (own(in_weights), own(out_weights), own(skip))
-    cells = frames * side * side
-    _, states_b, mixed, pooled = forward(maps, in_w, out_w, decay_v, skip_v[None])
-    gathered = jnp.sum(gather(pooled), axis=2) / cells
-    gathered = gathered.reshape(rings, 2, clips, channels).transpose(1, 0, 2, 3)
-    dpooled = middle(gathered.reshape(-1, channels), proj_in, proj_gain, proj_out)
-    row = (view * rings + ring) * clips + clip
-    dpool = lax.dynamic_slice_in_dim(dpooled, row, 1, 0) / cells
-    grads = backward(maps, states_b, mixed, dpool, out_w, decay_v, skip_v[None])
+    states_b, slope, pooled = forward(maps, in_weights, out_weights, decays, skip)
+    dpooled = middle(gather(pooled), frames * side * side, proj_in, proj_gain, proj_out)
+    grads = backward(maps, states_b, slope, dpooled, out_weights, decays, skip)
     whole = reduce_grads(grads.reshape(-1, channels)).astype(jnp.float32)
     whole = whole.reshape(2, 2, 9 * channels, channels)
     return (whole[:, 0], whole[:, 1])

time: 197 us -> 188 us (0.954)
  other arithmetic: 6.44 us -> 1.42 us
  local copies, waits for them, and re-layouts: 4.68 us -> 1.57 us
    concatenate x3 -> x0, other arithmetic: 2.85 us -> none  [pair_weights(): jnp.concatenate([upper, lower], axis=-1)]
    pallas_call x1, Pallas kernels: 44.5 us -> 42.5 us  [backward(): pl.pallas_call(backward_kernel, grid=(steps,), in_specs=[frame_spec, fram...]
where the time goes in v2:
time: 188 us; the launch traced here: 187 us
  Pallas kernels  184 us (98%)
    pallas_call x1, Pallas kernels, exchange(): pl.pallas_call(exchange_kernel, in_specs=[pl.BlockSpec(memory_space=pl.AN...  50.3 us
    pallas_call x1, Pallas kernels, backward(): pl.pallas_call(backward_kernel, grid=(steps,), in_specs=[frame_spec, fram...  42.5 us
    pallas_call x1, Pallas kernels, reduce_grads(): pl.pallas_call(reduce_kernel, in_specs=[pl.BlockSpec(memory_space=pltpu.V...  35.6 us
    pallas_call x1, Pallas kernels, forward(): pl.pallas_call(forward_kernel, grid=(frames // BLOCK,), in_specs=[frame_s...  31.9 us
    pallas_call x1, Pallas kernels, gather(): pl.pallas_call(gather_kernel, in_specs=[pl.BlockSpec(memory_space=pltpu.V...  13 us
    pallas_call x1, Pallas kernels, middle(): pl.pallas_call(functools.partial(middle_kernel, cells), in_specs=[whole]...  10.3 us

profile of v2, /device:TPU:0, one launch (start us, length us, event | category | flops | bytes accessed | tf_op | source)
XLA Modules:
  0.0 187.4 jit_solution(16761888101576802384)
XLA Ops:
  0.6 50.3 %shard_map.104 = (bf16[64,16,16,128]{3,2,1,0:T(8,128)(2,1)}, f32[64,128]{1,0:T(8,128)}) custom-call(bf16[4,8,16,16,128]{4,3,2,1,0:T(8,128)(2,1)} %rgb.1, bf16[4,8,16,16,128]{4,3,2,1,0:T(8,128)(2,1)} %flow.1, f32[2,8,128]{2,1,0:T(8,128)} %decay.1), custom_call_target="tpu_custom_call" | custom-call | tf_op jit(solution)/shard_map/pallas_call | solution.py:371
  51.0 31.9 %shard_map.105 = (bf16[64,8,2,16,128]{4,3,2,1,0:T(8,128)(2,1)}, f32[64,8,2,16,128]{4,3,2,1,0:T(8,128)}, f32[8,128]{1,0:T(8,128)}) custom-call(bf16[64,8,2,16,128]{4,3,2,1,0:T(8,128)(2,1)} %bitcast.14, bf16[2,1152,128]{2,1,0:T(8,128)(2,1)} %in_w.1, bf16[2,1152,128]{2,1,0:T(8,128)(2,1)} %out_w.3, f32[64,128]{1,0:T(8,128)} %get-tuple-element.8.decay, f32[2,128]{1,0:T(2,128)} %skip.3), custom_call_target="tpu_custom_call" | custom-call | tf_op jit(solution)/shard_map/pallas_call | solution.py:752
  82.9 13.0 %shard_map.106.everyone = f32[4,8,8,128]{3,2,1,0:T(8,128)} custom-call(f32[8,128]{1,0:T(8,128)} %get-tuple-element.11.pooled), custom_call_target="tpu_custom_call" | custom-call | tf_op jit(solution)/shard_map/pallas_call | solution.py:416
  95.9 10.3 %shard_map.107.dpooled = f32[32,128]{1,0:T(8,128)} custom-call(f32[4,8,8,128]{3,2,1,0:T(8,128)} %shard_map.106.everyone, f32[128,2048]{1,0:T(8,128)} %proj_in.1, f32[1,2048]{1,0:T(1,128)} %bitcast.17, bf16[2048,2048]{1,0:T(8,128)(2,1)} %proj_out.1), custom_call_target="tpu_custom_call" | custom-call | tf_op jit(solution)/shard_map/pallas_call | solution.py:805
  106.2 42.5 %shard_map.108 = f32[2,1152,128]{2,1,0:T(8,128)} custom-call(bf16[64,8,2,16,128]{4,3,2,1,0:T(8,128)(2,1)} %bitcast.15, bf16[64,8,2,16,128]{4,3,2,1,0:T(8,128)(2,1)} %get-tuple-element.9.states_b, f32[64,8,2,16,128]{4,3,2,1,0:T(8,128)} %get-tuple-element.10.slope, f32[32,128]{1,0:T(8,128)} %shard_map.107.dpooled, bf16[2,1152,128]{2,1,0:T(8,128)(2,1)} %out_w.3, ...), custom_call_target="tpu_custom_call" | custom-call | tf_op jit(solution)/shard_map/pallas_call | solution.py:785
  148.7 35.6 %shard_map.109 = bf16[2,2,2,4,144,128]{5,4,3,2,1,0:T(8,128)(2,1)} custom-call(f32[2,2,4,144,128]{4,3,2,1,0:T(8,128)} %bitcast.16), custom_call_target="tpu_custom_call" | custom-call | tf_op jit(solution)/shard_map/pallas_call | solution.py:496
  184.4 1.4 bitcast_convert_fusion
  185.8 1.6 slice_bitcast_fusion

commit v3 on v2

--- a/solution.py
+++ b/solution.py
@@ -302,8 +302,12 @@
     return (whole[0], whole[1])
 
 
-BLOCK = 8
-VMEM_BYTES = 56 * 1024 * 1024
+BLOCK = 16
+PARTS = 4
+FORWARD_BYTES = 20 * 1024 * 1024
+MIDDLE_BYTES = 16 * 1024 * 1024
+BACKWARD_BYTES = 24 * 1024 * 1024
+SMALL_BYTES = 4 * 1024 * 1024
 
 
 MESH = pl.DeviceIdType.MESH
@@ -370,14 +374,16 @@
     others = pltpu.SemaphoreType.DMA((peers - 1,))
     return pl.pallas_call(
         exchange_kernel,
-        in_specs=[pl.BlockSpec(memory_space=pl.ANY)] * 3,
+        in_specs=[pl.BlockSpec(memory_space=pltpu.HBM)] * 3,
         out_specs=[pl.BlockSpec(memory_space=pl.ANY)] * 2,
         out_shape=[
             jax.ShapeDtypeStruct((frames * peers,) + rgb_maps.shape[2:], rgb_maps.dtype),
             jax.ShapeDtypeStruct((frames * peers, channels), decay.dtype),
         ],
         scratch_shapes=[others, others, others, others, pltpu.SemaphoreType.DMA((2,))],
-        compiler_params=pltpu.CompilerParams(collective_id=0, has_side_effects=True),
+        compiler_params=pltpu.CompilerParams(
+            collective_id=0, has_side_effects=True, vmem_limit_bytes=SMALL_BYTES
+        ),
     )(rgb_maps, flow_maps, decay)
 
 
@@ -419,11 +425,13 @@
         out_specs=pl.BlockSpec(memory_space=pltpu.VMEM),
         out_shape=jax.ShapeDtypeStruct((rings, peers) + pooled.shape, pooled.dtype),
         scratch_shapes=[count, count],
-        compiler_params=pltpu.CompilerParams(collective_id=1, has_side_effects=True),
+        compiler_params=pltpu.CompilerParams(
+            collective_id=1, has_side_effects=True, vmem_limit_bytes=SMALL_BYTES
+        ),
     )(pooled)
 
 
-def reduce_kernel(grads, whole, from_core, to_x, from_x, acc, from_ring, send, recv):
+def reduce_kernel(grads, whole, from_core, to_x, from_x, acc, to_ring, from_ring, send, recv):
     me, ring, rings = (lax.axis_index("tm"), lax.axis_index("batch"), lax.axis_size("batch"))
     core, x, y = (lax.rem(me, 2), lax.rem(me // 2, 2), me // 4)
     sibling, across, beyond = (
@@ -452,19 +460,21 @@
     passed = push(grads.at[1 - core, 1 - x], from_core.at[0], sibling)
     kept = push(grads.at[1 - core, x], from_core.at[1], sibling)
     passed.wait_recv()
-    to_x[...] = grads[core, 1 - x] + from_core[0]
+    to_x[...] = (grads[core, 1 - x] + from_core[0]).astype(to_x.dtype)
     crossed = push(to_x, from_x, across)
     kept.wait_recv()
     acc[...] = grads[core, x] + from_core[1]
     crossed.wait_recv()
-    acc[...] += from_x[...]
+    acc[...] += from_x[...].astype(jnp.float32)
+    to_ring[...] = acc[...].astype(to_ring.dtype)
     arrivals = [
-        push(acc.at[other], from_ring.at[k], {"batch": other}) for k, other in enumerate(others)
+        push(to_ring.at[other], from_ring.at[k], {"batch": other})
+        for k, other in enumerate(others)
     ]
     total = acc[ring]
     for k, copy in enumerate(arrivals):
         copy.wait_recv()
-        total = total + from_ring[k]
+        total = total + from_ring[k].astype(jnp.float32)
     whole[y, core, x, ring] = total.astype(whole.dtype)
     part = whole.at[y, core, x, ring]
     for copy in [push(part, part, {"batch": other}) for other in others]:
@@ -500,15 +510,16 @@
         out_shape=jax.ShapeDtypeStruct((2, 2, 2) + part, jnp.bfloat16),
         scratch_shapes=[
             pltpu.VMEM((2,) + part, jnp.float32),
+            pltpu.VMEM(part, jnp.bfloat16),
+            pltpu.VMEM(part, jnp.bfloat16),
             pltpu.VMEM(part, jnp.float32),
-            pltpu.VMEM(part, jnp.float32),
-            pltpu.VMEM(part, jnp.float32),
-            pltpu.VMEM((rings - 1,) + part[1:], jnp.float32),
+            pltpu.VMEM(part, jnp.bfloat16),
+            pltpu.VMEM((rings - 1,) + part[1:], jnp.bfloat16),
             count,
             count,
         ],
         compiler_params=pltpu.CompilerParams(
-            collective_id=2, has_side_effects=True, vmem_limit_bytes=VMEM_BYTES
+            collective_id=2, has_side_effects=True, vmem_limit_bytes=MIDDLE_BYTES
         ),
     )(grads.reshape((2, 2) + part))
 
@@ -579,7 +590,8 @@
     pooled,
     in_pairs,
     out_pairs,
-    padded,
+    padded_in,
+    padded_out,
     inputs,
     carried,
 ):
@@ -590,29 +602,36 @@
     def _():
         put_pairs(in_pairs, tap_reader(in_w, view))
         put_pairs(out_pairs, tap_reader(out_w, view))
-        clear_edges(padded)
+        for at in range(PARTS):
+            clear_edges(padded_in.at[at])
+            clear_edges(padded_out.at[at])
         carried[...] = jnp.zeros_like(carried)
         pooled[...] = jnp.zeros_like(pooled)
 
-    for frame in range(maps.shape[0]):
-        put_shifts(padded, frame, maps[frame])
-    even, odd = conv_rows(padded, in_pairs)
-    inputs[:, :, 0] = even.astype(jnp.bfloat16)
-    inputs[:, :, 1] = odd.astype(jnp.bfloat16)
-    for frame in range(maps.shape[0]):
-        now = decay[frame : frame + 1, :].reshape(1, 1, 1, -1)
-        state = now * carried[...] + inputs[frame].astype(jnp.float32)
-        carried[...] = state
-        states_b[frame] = put_shifts(padded, frame, state)
+    size = maps.shape[0] // PARTS
+    parts = [slice(at * size, (at + 1) * size) for at in range(PARTS)]
     gain = skip[pl.ds(view, 1), :].reshape(1, 1, 1, -1)
-    total = pooled[...]
-    for parity, out in enumerate(conv_rows(padded, out_pairs)):
-        value = out + gain * inputs[:, :, parity].astype(jnp.float32)
-        sigma = sigmoid(value)
-        active = value * sigma
-        slope[:, :, parity] = sigma + active * (1.0 - sigma)
-        total = total + jnp.sum(active.reshape(-1, 8, active.shape[-1]), axis=0)
-    pooled[...] = total
+    for at, part in enumerate(parts):
+        for frame in range(size):
+            put_shifts(padded_in.at[at], frame, maps[part.start + frame])
+        even, odd = conv_rows(padded_in.at[at], in_pairs)
+        inputs[part, :, 0] = even.astype(jnp.bfloat16)
+        inputs[part, :, 1] = odd.astype(jnp.bfloat16)
+    state = carried[...]
+    for at, part in enumerate(parts):
+        for frame in range(size):
+            here = part.start + frame
+            now = decay[here : here + 1, :].reshape(1, 1, 1, -1)
+            state = now * state + inputs[here].astype(jnp.float32)
+            states_b[here] = put_shifts(padded_out.at[at], frame, state)
+        mixed = conv_rows(padded_out.at[at], out_pairs)
+        for parity, out in enumerate(mixed):
+            value = out + gain * inputs[part, :, parity].astype(jnp.float32)
+            sigma = sigmoid(value)
+            active = value * sigma
+            slope[part, :, parity] = sigma + active * (1.0 - sigma)
+            pooled[...] += jnp.sum(active.reshape(-1, 8, active.shape[-1]), axis=0)
+    carried[...] = state
 
 
 def backward_kernel(
@@ -625,7 +644,8 @@
     skip,
     grads,
     pairs,
-    padded,
+    padded_out,
+    padded_in,
     dmix,
     total,
     carried,
@@ -640,11 +660,13 @@
     def _():
         read = tap_reader(out_w, view)
         put_pairs(pairs, lambda k: read(8 - k).astype(jnp.float32).T.astype(jnp.bfloat16))
-        clear_edges(padded)
+        for at in range(PARTS):
+            clear_edges(padded_in.at[at])
+            clear_edges(padded_out.at[at])
         carried[...] = jnp.zeros_like(carried)
         total[...] = jnp.zeros_like(total)
 
-    def tap_product(values):
+    def tap_product(values, padded):
         both = jnp.concatenate([values[:, :, 0], values[:, :, 1]], axis=-1)
         return lax.dot_general(
             both.reshape(-1, 2 * channels),
@@ -656,21 +678,32 @@
     row = lax.axis_index("batch") * peers + me
     share = (dpooled[pl.ds(row, 1), :] / (frames * 2 * half * side)).reshape(1, 1, 1, -1)
     gain = skip[pl.ds(view, 1), :].reshape(1, 1, 1, -1)
-    for frame in range(block):
-        part = share * slope[frame]
-        dmix[frame] = gain * part
-        put_shifts(padded, frame, part)
-    total[1] += tap_product(states_b[...])
-    even, odd = conv_rows(padded, pairs)
+    size = block // PARTS
+    parts = [(at, slice(at * size, (at + 1) * size)) for at in reversed(range(PARTS))]
     first = (steps - 1 - step) * block
-    for frame in reversed(range(block)):
-        now = decay[pl.ds(jnp.minimum(first + frame + 1, frames - 1), 1), :].reshape(1, 1, -1)
-        for parity, out in enumerate((even, odd)):
-            adjoint = out[frame] + now * carried[:, parity]
-            carried[:, parity] = adjoint
-            dmix[frame, :, parity] += adjoint
-        put_shifts(padded, frame, dmix[frame])
-    total[0] += tap_product(maps[...])
+    outs = []
+    for at, part in parts:
+        for frame in range(size):
+            here = part.start + frame
+            mixed = share * slope[here]
+            dmix[here] = gain * mixed
+            put_shifts(padded_out.at[at], frame, mixed)
+        outs.append(conv_rows(padded_out.at[at], pairs))
+    back = [carried[:, parity] for parity in range(2)]
+    for (at, part), out in zip(parts, outs):
+        total[1] += tap_product(states_b[part], padded_out.at[at])
+        for frame in reversed(range(size)):
+            here = part.start + frame
+            row = jnp.minimum(first + here + 1, frames - 1)
+            now = decay[pl.ds(row, 1), :].reshape(1, 1, -1)
+            for parity in range(2):
+                back[parity] = out[parity][frame] + now * back[parity]
+                dmix[here, :, parity] += back[parity]
+            put_shifts(padded_in.at[at], frame, dmix[here])
+    for parity in range(2):
+        carried[:, parity] = back[parity]
+    for at, part in parts:
+        total[0] += tap_product(maps[part], padded_in.at[at])
 
     @pl.when(step == steps - 1)
     def _():
@@ -741,6 +774,10 @@
         precision=HIGHEST,
         preferred_element_type=jnp.float32,
     )
+
+
+def padded_shape(half, side, channels):
+    return pltpu.VMEM((PARTS, BLOCK // PARTS, half + 1, 2, side, 3 * channels), jnp.bfloat16)
 
 
 def forward(maps, in_w, out_w, decay, skip):
@@ -768,11 +805,12 @@
         scratch_shapes=[
             pairs,
             pairs,
-            pltpu.VMEM((BLOCK, half + 1, 2, side, 3 * channels), jnp.bfloat16),
+            padded_shape(half, side, channels),
+            padded_shape(half, side, channels),
             pltpu.VMEM(shape, jnp.bfloat16),
             pltpu.VMEM(shape[1:], jnp.float32),
         ],
-        compiler_params=pltpu.CompilerParams(vmem_limit_bytes=VMEM_BYTES),
+        compiler_params=pltpu.CompilerParams(vmem_limit_bytes=FORWARD_BYTES),
     )(maps, in_w, out_w, decay, skip)
 
 
@@ -790,12 +828,13 @@
         out_shape=jax.ShapeDtypeStruct((2, 9 * channels, channels), jnp.float32),
         scratch_shapes=[
             pltpu.VMEM((12 * channels, 2 * channels), jnp.bfloat16),
-            pltpu.VMEM((BLOCK, half + 1, 2, side, 3 * channels), jnp.bfloat16),
+            padded_shape(half, side, channels),
+            padded_shape(half, side, channels),
             pltpu.VMEM(shape, jnp.float32),
             pltpu.VMEM((2, 2 * channels, 12 * channels), jnp.float32),
             pltpu.VMEM(shape[1:], jnp.float32),
         ],
-        compiler_params=pltpu.CompilerParams(vmem_limit_bytes=VMEM_BYTES),
+        compiler_params=pltpu.CompilerParams(vmem_limit_bytes=BACKWARD_BYTES),
     )(maps, states_b, slope, dpooled, out_w, decay, skip)
 
 
@@ -807,7 +846,7 @@
         in_specs=[whole] * 4,
         out_specs=whole,
         out_shape=jax.ShapeDtypeStruct((rings * peers, channels), jnp.float32),
-        compiler_params=pltpu.CompilerParams(vmem_limit_bytes=VMEM_BYTES),
+        compiler_params=pltpu.CompilerParams(vmem_limit_bytes=MIDDLE_BYTES),
     )(everyone, proj_in, proj_gain[None], proj_out)
 
 

time: 188 us -> 146 us (0.78)
  Pallas kernels: 184 us -> 137 us
  local copies, waits for them, and re-layouts: 1.57 us -> 8.24 us
    pallas_call x1, Pallas kernels: 42.5 us -> 23.4 us  [backward(): pl.pallas_call(backward_kernel, grid=(steps,), in_specs=[frame_spec, fram...]
    pallas_call x1, Pallas kernels: 31.9 us -> 18.3 us  [forward(): pl.pallas_call(forward_kernel, grid=(frames // BLOCK,), in_specs=[frame_s...]
    pallas_call x1, Pallas kernels: 35.6 us -> 27.2 us  [reduce_grads(): pl.pallas_call(reduce_kernel, in_specs=[pl.BlockSpec(memory_space=pltpu.V...]
    unnamed x0 -> x20, local copies, waits for them, and re-layouts: none -> 6.69 us
    pallas_call x1, Pallas kernels: 10.3 us -> 5.98 us  [middle(): pl.pallas_call(functools.partial(middle_kernel, cells), in_specs=[whole]...]
where the time goes in v3:
time: 146 us
  Pallas kernels  137 us (94%)
  local copies, waits for them, and re-layouts  8.24 us (6%)
    pallas_call x1, Pallas kernels, exchange(): pl.pallas_call(exchange_kernel, in_specs=[pl.BlockSpec(memory_space=pltpu...  50.1 us
    pallas_call x1, Pallas kernels, reduce_grads(): pl.pallas_call(reduce_kernel, in_specs=[pl.BlockSpec(memory_space=pltpu.V...  27.2 us
    pallas_call x1, Pallas kernels, backward(): pl.pallas_call(backward_kernel, grid=(steps,), in_specs=[frame_spec, fram...  23.4 us
    pallas_call x1, Pallas kernels, forward(): pl.pallas_call(forward_kernel, grid=(frames // BLOCK,), in_specs=[frame_s...  18.3 us
    pallas_call x1, Pallas kernels, gather(): pl.pallas_call(gather_kernel, in_specs=[pl.BlockSpec(memory_space=pltpu.V...  11.7 us
    unnamed x20, local copies, waits for them, and re-layouts  6.69 us
    pallas_call x1, Pallas kernels, middle(): pl.pallas_call(functools.partial(middle_kernel, cells), in_specs=[whole]...  5.98 us

profile of v3, /device:TPU:0, one launch (start us, length us, event | category | flops | bytes accessed | tf_op | source)
XLA Modules:
  0.0 145.9 jit_solution(11710821526363379170)
XLA Ops:
  0.6 0.0 copy-start.3
  0.6 1.6 %copy-done.3 = bf16[4,8,16,16,128]{4,3,2,1,0:T(8,128)(2,1)S(1)} copy-done((bf16[4,8,16,16,128]{4,3,2,1,0:T(8,128)(2,1)S(1)}, bf16[4,8,16,16,128]{4,3,2,1,0:T(8,128)(2,1)}, u32[]{:S(2)}) %copy-start.3) | copy-done | bytes 2097176
  2.2 0.0 copy-start.4
  2.2 1.6 %copy-done.4 = bf16[4,8,16,16,128]{4,3,2,1,0:T(8,128)(2,1)S(1)} copy-done((bf16[4,8,16,16,128]{4,3,2,1,0:T(8,128)(2,1)S(1)}, bf16[4,8,16,16,128]{4,3,2,1,0:T(8,128)(2,1)}, u32[]{:S(2)}) %copy-start.4) | copy-done | bytes 2097176
  3.8 0.0 copy-start.7
  3.8 0.7 copy-done.7
  4.5 0.0 copy-start
  4.5 50.1 %shard_map.104 = (bf16[64,16,16,128]{3,2,1,0:T(8,128)(2,1)S(1)}, f32[64,128]{1,0:T(8,128)S(1)}) custom-call(bf16[4,8,16,16,128]{4,3,2,1,0:T(8,128)(2,1)S(1)} %copy-done.3, bf16[4,8,16,16,128]{4,3,2,1,0:T(8,128)(2,1)S(1)} %copy-done.4, f32[2,8,128]{2,1,0:T(8,128)S(1)} %copy-done.7), custom_call_target="tpu_custom_call" | custom-call | tf_op jit(solution)/shard_map/pallas_call | solution.py:375
  54.6 0.0 copy-start.1
  54.6 1.1 copy-done.1
  55.7 0.0 copy-start.6
  55.7 1.1 copy-done.6
  56.7 0.0 copy-start.9
  56.7 0.7 copy-done.9
  57.4 0.0 copy-start.5
  57.4 0.0 copy-start.8
  57.4 18.3 %shard_map.105 = (bf16[64,8,2,16,128]{4,3,2,1,0:T(8,128)(2,1)S(1)}, f32[64,8,2,16,128]{4,3,2,1,0:T(8,128)S(1)}, f32[8,128]{1,0:T(8,128)S(1)}) custom-call(bf16[64,8,2,16,128]{4,3,2,1,0:T(8,128)(2,1)S(1)} %bitcast.14, bf16[2,1152,128]{2,1,0:T(8,128)(2,1)S(1)} %copy-done.6, bf16[2,1152,128]{2,1,0:T(8,128)(2,1)S(1)} %copy-done.1, ...), custom_call_target="tpu_custom_call" | custom-call | tf_op jit(solution)/shard_map/pallas_call | solution.py:789
  75.8 11.7 %shard_map.106.everyone = f32[4,8,8,128]{3,2,1,0:T(8,128)S(1)} custom-call(f32[8,128]{1,0:T(8,128)S(1)} %get-tuple-element.11.pooled), custom_call_target="tpu_custom_call" | custom-call | tf_op jit(solution)/shard_map/pallas_call | solution.py:422
  87.5 0.0 copy-done
  87.5 0.0 copy-done.5
  87.5 0.0 copy-done.8
  87.5 0.0 copy-start.2
  87.5 6.0 %shard_map.107.dpooled = f32[32,128]{1,0:T(8,128)S(1)} custom-call(f32[4,8,8,128]{3,2,1,0:T(8,128)S(1)} %shard_map.106.everyone, f32[128,2048]{1,0:T(8,128)S(1)} %copy-done.5, f32[1,2048]{1,0:T(1,128)S(1)} %bitcast.17, bf16[2048,2048]{1,0:T(8,128)(2,1)S(1)} %copy-done), custom_call_target="tpu_custom_call" | custom-call | tf_op jit(solution)/shard_map/pallas_call | solution.py:844
  93.5 0.0 copy-done.2
  93.5 23.4 %shard_map.108 = f32[2,1152,128]{2,1,0:T(8,128)S(1)} custom-call(bf16[64,8,2,16,128]{4,3,2,1,0:T(8,128)(2,1)S(1)} %bitcast.15, bf16[64,8,2,16,128]{4,3,2,1,0:T(8,128)(2,1)S(1)} %get-tuple-element.9.states_b, f32[64,8,2,16,128]{4,3,2,1,0:T(8,128)S(1)} %get-tuple-element.10.slope, f32[32,128]{1,0:T(8,128)S(1)} %shard_map.107.dpooled, ...), custom_call_target="tpu_custom_call" | custom-call | tf_op jit(solution)/shard_map/pallas_call | solution.py:823
  116.9 27.2 %shard_map.109 = bf16[2,2,2,4,144,128]{5,4,3,2,1,0:T(8,128)(2,1)S(1)} custom-call(f32[2,2,4,144,128]{4,3,2,1,0:T(8,128)S(1)} %bitcast.16), custom_call_target="tpu_custom_call" | custom-call | tf_op jit(solution)/shard_map/pallas_call | solution.py:506
  144.1 0.2 bitcast_convert_fusion
  144.3 1.6 %slice_bitcast_fusion = (f32[2,1152,128]{2,1,0:T(8,128)}, f32[2,1152,128]{2,1,0:T(8,128)}) fusion(f32[2,2,1152,128]{3,2,1,0:T(8,128)S(1)} %bitcast_convert_fusion), kind=kLoop, calls=%fused_computation | loop fusion | bytes 4718592 | tf_op jit(solution)/shard_map/squeeze | solution.py:865
Async XLA Ops:
  0.6 1.6 %copy-start.3 = (bf16[4,8,16,16,128]{4,3,2,1,0:T(8,128)(2,1)S(1)}, bf16[4,8,16,16,128]{4,3,2,1,0:T(8,128)(2,1)}, u32[]{:S(2)}) copy-start(bf16[4,8,16,16,128]{4,3,2,1,0:T(8,128)(2,1)} %rgb.1) | copy-start | bytes 6291460
  2.2 1.6 %copy-start.4 = (bf16[4,8,16,16,128]{4,3,2,1,0:T(8,128)(2,1)S(1)}, bf16[4,8,16,16,128]{4,3,2,1,0:T(8,128)(2,1)}, u32[]{:S(2)}) copy-start(bf16[4,8,16,16,128]{4,3,2,1,0:T(8,128)(2,1)} %flow.1) | copy-start | bytes 6291460
  3.8 0.7 copy-start.7
  4.5 83.0 %copy-start = (bf16[2048,2048]{1,0:T(8,128)(2,1)S(1)}, bf16[2048,2048]{1,0:T(8,128)(2,1)}, u32[]{:S(2)}) copy-start(bf16[2048,2048]{1,0:T(8,128)(2,1)} %proj_out.1) | copy-start | bytes 25165828
  54.6 1.1 copy-start.1
  55.7 1.1 copy-start.6
  56.7 0.7 copy-start.9
  57.4 30.1 %copy-start.5 = (f32[128,2048]{1,0:T(8,128)S(1)}, f32[128,2048]{1,0:T(8,128)}, u32[]{:S(2)}) copy-start(f32[128,2048]{1,0:T(8,128)} %proj_in.1) | copy-start | bytes 3145732
  57.4 30.1 %copy-start.8 = (f32[2048]{0:T(1024)S(1)}, f32[2048]{0:T(1024)}, u32[]{:S(2)}) copy-start(f32[2048]{0:T(1024)} %param.16) | copy-start | bytes 24580
  87.5 6.0 %copy-start.2 = (bf16[2,1152,128]{2,1,0:T(8,128)(2,1)S(1)}, bf16[2,1152,128]{2,1,0:T(8,128)(2,1)}, u32[]{:S(2)}) copy-start(bf16[2,1152,128]{2,1,0:T(8,128)(2,1)} %out_w.3) | copy-start | bytes 1769476
